TPU v7x, 1024 devices: a whole 4x4x32 slice. The times are simulated.
1024 devices in a mesh: row: 8 (over z_hi, core), col: 128 (over y, x, z_lo).
Axes of the slice: x: 4, y: 4, z: 32 (z_hi: 4, z_lo: 8; z = z_hi * 8 + z_lo), core: 2. Of those that a mesh axis runs over, the one named last changes fastest.
Arguments:
- strip_factors: bfloat16 [32768, 64], P(('row', 'col')), may hold values from -8 to 8
- sku_factors: bfloat16 [262144, 64], P('col', 'row'), may hold values from -8 to 8
- probe: bfloat16 [262144, 16], P('col', 'row'), may hold values from -6 to 6
- demand_weight: float32 [1, 32768], P(None, ('row', 'col')), may hold values from 1 to 30, as said below
Outputs:
- basis: float32 [16, 32768], P(None, ('row', 'col'))
Inputs may be any that keep to these rules, and one draw needn't show every extreme that they name: `demand_weight`: positive weights.
All inputs are finite; a program needn't handle non-finite values.
Results may differ from a plain program's by a relative error of at most 0.009.
The roundings to bfloat16 on the way count: a program that leaves them out, or rounds other values in their place, can miss the bound.
Values may be sent and summed in bfloat16 or wider, within the bound.
No kernel may reach another device: no remote copies, remote signals or barrier semaphores. Data moves between devices by JAX's collectives and lax.ppermute only.
A program may use at most 32 MiB of HBM per device.

v0:
```python
import jax
import jax.numpy as jnp
from jax import lax
from jax.sharding import PartitionSpec as P


def unit_rows(factors):
    wide = factors.astype(jnp.float32)
    scale = lax.rsqrt(jnp.sum(wide * wide, axis=1, keepdims=True) + 1e-06)
    return (wide * scale).astype(jnp.bfloat16)


def per_device(strip_factors, sku_factors, probe, demand_weight):
    strip_unit = unit_rows(strip_factors)
    panel_raw, probe_cols = (
        lax.all_gather(sku_factors, "row", axis=1, tiled=True),
        lax.all_gather(probe, "row", axis=1, tiled=True),
    )
    sku_unit = unit_rows(panel_raw)
    columns = sku_unit.shape[0]
    width = min(512, columns)
    count = columns // width
    piece = lax.all_gather(strip_unit, "col", axis=0, tiled=True)
    total = jnp.zeros((probe_cols.shape[1], piece.shape[0]), jnp.float32)
    for number in range(count):
        panel = sku_unit[number * width : (number + 1) * width]
        block_probe = probe_cols[number * width : (number + 1) * width]
        corr = lax.dot_general(
            piece, panel, (((1,), (1,)), ((), ())), preferred_element_type=jnp.float32
        )
        affinity = jnp.exp(corr).astype(jnp.bfloat16)
        total = total + lax.dot_general(
            block_probe, affinity, (((0,), (1,)), ((), ())), preferred_element_type=jnp.float32
        )
    image = lax.psum_scatter(total, "col", scatter_dimension=1, tiled=True)
    local_gram = jnp.dot(image * demand_weight, image.T, precision=lax.Precision.HIGHEST)
    gram = lax.psum(local_gram, ("row", "col"))
    lower = jnp.linalg.cholesky(gram)
    return jax.scipy.linalg.solve_triangular(lower, image, lower=True)


def solution(mesh):
    placed = (P(("row", "col"), None), P("col", "row"), P("col", "row"), P(None, ("row", "col")))
    return jax.shard_map(
        per_device, mesh=mesh, in_specs=placed, out_specs=P(None, ("row", "col")), check_vma=False
    )
```

profile of v0, /device:TPU:1, one launch (start us, length us, event | category | flops | bytes accessed | tf_op | source)
XLA Modules:
  0.0 1833.3 jit_solution(7252891062964497934)
XLA Ops:
  6.5 0.0 reduce-scatter.4.cloned.1.call-start
  6.5 0.8 fusion.12
  7.4 0.8 fusion.13
  8.1 46.2 %all-gather = bf16[8,2,2048]{2,1,0:T(2,128)(2,1)S(1)} all-gather(bf16[1,2,2048]{2,1,0:T(2,128)(2,1)} %bitcast.32), channel_id=1, replica_groups=mesh['row'=8,'col'=128] {'row'}, dimensions={0}, use_global_device_ids=true | all-gather | bytes 73728 | tf_op jit(solution)/shard_map/all_gather | solution.py:17
  54.3 29.2 %all_gather.10 = bf16[2048,64]{0,1:T(8,128)(2,1)S(1)} all-gather(bf16[2048,8]{0,1:T(8,128)(2,1)} %param.5), channel_id=1, replica_groups=mesh['row'=8,'col'=128] {'row'}, dimensions={1}, use_global_device_ids=true | all-gather | bytes 294912 | tf_op jit(solution)/shard_map/all_gather | solution.py:16
  83.5 0.1 fusion.2
  83.7 470.3 %all_gather.9 = bf16[4096,64]{1,0:T(8,128)(2,1)S(1)} all-gather(bf16[32,64]{1,0:T(8,128)(2,1)S(1)} %fusion.13), channel_id=1, replica_groups=mesh['row'=8,'col'=128] {'col'}, dimensions={0}, use_global_device_ids=true | all-gather | bytes 528384 | tf_op jit(solution)/shard_map/all_gather | solution.py:23
  554.0 2.2 fusion.1
  556.2 2.3 convolution_add_fusion.2
  558.4 2.2 convolution_add_fusion.1
  560.7 2.2 fusion
  562.9 0.0 copy-start
  562.9 2.0 copy.10
  564.9 0.0 reduce-scatter.4.cloned.1.call-update
  564.9 994.7 %reduce-scatter.4.cloned.1.call-done = f32[32,16]{1,0:T(8,128)} async-done(((f32[4096,16]{1,0:T(8,128)}), f32[32,16]{1,0:T(8,128)}) %reduce-scatter.4.cloned.1.call-update) | async-done | bytes 2064
  1559.7 0.8 copy.11
  1560.5 0.0 copy-done
  1560.5 0.9 fusion.22
  1561.4 259.4 %psum.7 = f32[16,16]{0,1:T(8,128)S(1)} all-reduce(f32[16,16]{0,1:T(8,128)S(1)} %fusion.22), channel_id=1, replica_groups=mesh['row'=8,'col'=128] {'row','col'}, use_global_device_ids=true, to_apply=%region_3.0 | all-reduce | flops 256 | bytes 2048 | tf_op jit(solution)/shard_map/psum | solution.py:37
  1820.8 0.1 copy.8
  1820.9 1.5 cholesky.16
  1822.3 0.6 compare_reduce_fusion
  1823.0 0.6 fusion.18
  1823.7 1.2 custom-call.7
  1824.9 1.5 fusion.19
  (6 shorter events, 0.1 us)
Async XLA Ops:
  6.5 1553.2 %reduce-scatter.4.cloned.1.call-start = ((), (), s32[]{:S(2)}) async-start(), calls=%async_computation.1 | async-start | bytes 2113536
  562.9 997.5 %copy-start = (f32[1,32]{1,0:T(1,128)S(1)}, f32[1,32]{1,0:T(1,128)}, u32[]{:S(2)}) copy-start(f32[1,32]{1,0:T(1,128)} %param.7) | copy-start | bytes 388
Sparse Core Ops, SparseCore 0:
  565.1 994.5 reduce-scatter.3
where the time goes:
time: 1830 us
  waiting for transfers between devices  995 us (54%)
  blocking collectives  805 us (44%)
    unnamed x2, waiting for transfers between devices  995 us
    all_gather x1, blocking collectives, per_device(): piece = lax.all_gather(strip_unit, 'col', axis=0, tiled=True)  470 us
    psum x1, blocking collectives, per_device(): gram = lax.psum(local_gram, ('row', 'col'))  259 us
    all_gather x1, blocking collectives, per_device(): lax.all_gather(probe, 'row', axis=1, tiled=True)  46.2 us
  transfers between devices with their start and end apart: 1, of which 1 were waited for; matrix products, arithmetic and copies ran while one was open for 0% of the time, Pallas kernels for 0%

commit v1 on v0

v1 whole, which is shorter than its diff:
```python
import jax
import jax.numpy as jnp
from jax import lax
from jax.experimental import pallas as pl
from jax.experimental.pallas import tpu as pltpu
from jax.sharding import Mesh
from jax.sharding import PartitionSpec as P

F32, BF16 = jnp.float32, jnp.bfloat16
AXES = ("z_hi", "core", "y", "x", "z_lo")
SIZES = (4, 2, 4, 4, 8)
ROW, COL = ("z_hi", "core"), ("y", "x", "z_lo")
VMEM = pl.BlockSpec(memory_space=pltpu.VMEM)
SMEM = pl.BlockSpec(memory_space=pltpu.SMEM)
T_STEP, S_STEP = 1024, 256


def kernel_call(body, outs, count, scratch=(), smem=0, name=None, **cost):
    return pl.pallas_call(
        body,
        out_shape=outs,
        in_specs=[SMEM] * smem + [VMEM] * (count - smem),
        out_specs=jax.tree.map(lambda _: VMEM, outs),
        scratch_shapes=list(scratch),
        name=name,
        compiler_params=pltpu.CompilerParams(vmem_limit_bytes=40 * 2**20),
    )


def shape(dims, kind=F32):
    return jax.ShapeDtypeStruct(dims, kind)


def pack_kernel(strip_ref, sku_ref, probe_ref, strips_ref, skus_ref):
    wide = strip_ref[...].astype(F32)
    scale = lax.rsqrt(jnp.sum(wide * wide, axis=1, keepdims=True) + 1e-06)
    unit = wide * scale
    packed = jnp.concatenate([unit[:16], unit[16:]], axis=1).astype(BF16)
    strips_ref[...] = jnp.broadcast_to(packed[None], strips_ref.shape)
    sku = sku_ref[...].astype(F32)
    probe = probe_ref[...].astype(F32)
    factors = jnp.concatenate([sku[:, :1024], sku[:, 1024:]], axis=0)
    columns = jnp.concatenate([probe[:, 256 * m : 256 * (m + 1)] for m in range(8)], axis=0)
    skus_ref[...] = jnp.concatenate([factors, columns], axis=1).astype(BF16)


def image_kernel(z_hi_ref, strips_ref, panel_ref, out_ref, wide_ref, columns_ref, unit_ref, turned_ref):
    z_hi = z_hi_ref[0]
    for back in range(4):
        place = lax.rem(z_hi + 4 - back, 4)
        for core in range(2):
            piece = panel_ref[core, back].astype(F32)
            wide_ref[place, core, :, :1024] = piece[:8, :1024]
            wide_ref[place, core, :, 1024:] = piece[8:, :1024]
            for m in range(8):
                columns_ref[place, core, :, 256 * m : 256 * (m + 1)] = piece[2 * m : 2 * m + 2, 1024:]
    wide = wide_ref[...].reshape(64, 2048)
    scale = lax.rsqrt(jnp.sum(wide * wide, axis=0, keepdims=True) + 1e-06)
    unit_ref[...] = (wide * scale).astype(BF16).T
    probe = jnp.concatenate([columns_ref[r // 2, r % 2] for r in range(8)], axis=0).astype(BF16)
    turned_ref[...] = strips_ref[...].T
    for half in range(2):
        for step in range(2048 // T_STEP):
            strip = turned_ref[64 * half : 64 * half + 64, T_STEP * step : T_STEP * (step + 1)]
            total = jnp.zeros((16, T_STEP), F32)
            for number in range(2048 // S_STEP):
                skus = slice(number * S_STEP, (number + 1) * S_STEP)
                corr = jnp.dot(unit_ref[skus, :], strip, preferred_element_type=F32)
                affinity = jnp.exp(corr).astype(BF16)
                total = total + jnp.dot(probe[:, skus], affinity, preferred_element_type=F32)
            for k in range(T_STEP // 128):
                out_ref[step * (T_STEP // 128) + k, 16 * half : 16 * half + 16, :] = total[:, 128 * k : 128 * (k + 1)]


def turn_kernel(parts_ref, out_ref):
    total = parts_ref[0]
    for k in range(1, parts_ref.shape[0]):
        total = total + parts_ref[k]
    turned = total.T.reshape(8, 16, 32)
    out_ref[...] = jnp.concatenate([turned[:, 4 * b : 4 * b + 4, :] for b in range(4)], axis=2)


def gram_kernel(parts_ref, weight_ref, image_ref, gram_ref):
    total = parts_ref[0]
    for k in range(1, parts_ref.shape[0]):
        total = total + parts_ref[k]
    turned = jnp.concatenate([total[:, 32 * b : 32 * b + 32] for b in range(4)], axis=0).T
    image = jnp.concatenate([turned[:16], turned[16:]], axis=1)
    image_ref[...] = image
    gram = lax.dot_general(
        image * weight_ref[...], image, (((1,), (1,)), ((), ())),
        precision=lax.Precision.HIGHEST, preferred_element_type=F32,
    )
    packed = jnp.concatenate([gram[:8], gram[8:], jnp.zeros((8, 96), F32)], axis=1)
    gram_ref[...] = jnp.broadcast_to(packed[None], gram_ref.shape)


def sum_kernel(parts_ref, out_ref):
    total = parts_ref[0]
    for k in range(1, parts_ref.shape[0]):
        total = total + parts_ref[k]
    out_ref[...] = jnp.broadcast_to(total[None], out_ref.shape)


def basis_kernel(parts_ref, image_ref, out_ref):
    total = parts_ref[0]
    for k in range(1, parts_ref.shape[0]):
        total = total + parts_ref[k]
    gram = jnp.concatenate([total[:, :16], total[:, 16:32]], axis=0)
    left = image_ref[...]
    rows = lax.broadcasted_iota(jnp.int32, (16, 1), 0)
    for k in range(15):
        below = rows > k
        ratio = jnp.where(below, gram[:, k : k + 1] / gram[k : k + 1, k : k + 1], 0.0)
        left = left - ratio * left[k : k + 1, :]
        gram = gram - ratio * gram[k : k + 1, :]
    diagonal = rows == lax.broadcasted_iota(jnp.int32, (16, 16), 1)
    pivots = jnp.sum(jnp.where(diagonal, gram, 0.0), axis=1, keepdims=True)
    out_ref[...] = left / jnp.sqrt(pivots)


def per_device(strip_factors, sku_factors, probe, demand_weight):
    strips, skus = kernel_call(
        pack_kernel, (shape((8, 16, 128), BF16), shape((16, 1280), BF16)), 3, name="pack"
    )(strip_factors, sku_factors.T, probe.T)
    shards = [skus] + [
        lax.ppermute(skus, "z_hi", [(i, (i + k) % 4) for i in range(4)]) for k in range(1, 4)
    ]
    strips = lax.all_to_all(strips, "z_lo", 0, 0, tiled=True).reshape(128, 128)
    strips = jnp.broadcast_to(strips[None], (16, 128, 128))
    strips = lax.all_to_all(strips, ("y", "x"), 0, 0, tiled=True).reshape(2048, 128)
    strips, *shards = lax.optimization_barrier((strips, *shards))
    panel = lax.all_gather(jnp.stack(shards), "core", axis=0)
    place = jnp.full((1,), lax.axis_index("z_hi"), jnp.int32)
    total = kernel_call(
        image_kernel, shape((16, 32, 128)), 3, smem=1, name="image",
        scratch=[pltpu.VMEM((4, 2, 8, 2048), F32), pltpu.VMEM((4, 2, 2, 2048), F32),
                 pltpu.VMEM((2048, 64), BF16), pltpu.VMEM((128, 2048), BF16)],
    )(place, strips, panel)
    total = lax.all_to_all(total, ("y", "x"), 0, 0, tiled=True)
    total = kernel_call(turn_kernel, shape((8, 4, 128)), 1, name="turn")(total)
    total = lax.all_to_all(total, "z_lo", 0, 0, tiled=True)
    image, gram = kernel_call(
        gram_kernel, (shape((16, 32)), shape((32, 8, 128))), 2, name="gram"
    )(total, demand_weight)
    gram = lax.all_to_all(gram, ("core", "y", "x"), 0, 0, tiled=True)
    gram = kernel_call(sum_kernel, shape((32, 8, 128)), 1, name="sum")(gram)
    gram = lax.all_to_all(gram, ("z_hi", "z_lo"), 0, 0, tiled=True)
    return kernel_call(basis_kernel, shape((16, 32)), 2, name="basis")(gram, image)


def solution(mesh):
    fine = Mesh(mesh.devices.reshape(SIZES), AXES)
    both = ROW + COL
    placed = (P(both, None), P(COL, ROW), P(COL, ROW), P(None, both))
    return jax.shard_map(
        per_device, mesh=fine, in_specs=placed, out_specs=P(None, both), check_vma=False
    )
```

time: 1830 us -> 177 us (0.10)
  waiting for transfers between devices: 995 us -> 13.1 us
  blocking collectives: 805 us -> 107 us
  starting transfers between devices: 0.01 us -> 41.9 us
    unnamed x2 -> x0, waiting for transfers between devices: 995 us -> none
    all_gather x3 -> x1, blocking collectives: 546 us -> 2.17 us  [per_device(): panel = lax.all_gather(jnp.stack(shards), 'core', axis=0)]
    psum x1 -> x0, blocking collectives: 259 us -> none  [per_device(): gram = lax.psum(local_gram, ('row', 'col'))]
    all_to_all x0 -> x5, blocking collectives: none -> 105 us  [the longest x1 40.7 us: per_device(): gram = lax.all_to_all(gram, ('z_hi', 'z_lo'), 0, 0, tiled=True)]
    ppermute x0 -> x3, starting transfers between devices: none -> 35.2 us  [per_device(): lax.ppermute(skus, 'z_hi', [(i, (i + k) % 4) for i in range(4)])]
  transfers between devices with their start and end apart: 1 -> 4, of which waited for: 1 -> 2; matrix products, arithmetic and copies ran while one was open for 0% -> 0% of each run, Pallas kernels for 0% -> 0%
where the time goes in v1:
time: 177 us
  blocking collectives  107 us (60%)
  starting transfers between devices  41.9 us (24%)
  waiting for transfers between devices  13.1 us (7%)
  Pallas kernels  11.6 us (7%)
  local copies, waits for them, and re-layouts  3.05 us (2%)
    all_to_all x1, blocking collectives, per_device(): gram = lax.all_to_all(gram, ('z_hi', 'z_lo'), 0, 0, tiled=True)  40.7 us
    ppermute x3, starting transfers between devices, per_device(): lax.ppermute(skus, 'z_hi', [(i, (i + k) % 4) for i in range(4)])  35.2 us
    all_to_all x1, blocking collectives, per_device(): strips = lax.all_to_all(strips, 'z_lo', 0, 0, tiled=True).reshape(128, 128)  22.4 us
    all_to_all x1, blocking collectives, per_device(): total = lax.all_to_all(total, ('y', 'x'), 0, 0, tiled=True)  14.7 us
    all_to_all x1, blocking collectives, per_device(): gram = lax.all_to_all(gram, ('core', 'y', 'x'), 0, 0, tiled=True)  13.4 us
    all_to_all x1, blocking collectives, per_device(): total = lax.all_to_all(total, 'z_lo', 0, 0, tiled=True)  13.3 us
    ppermute x3, waiting for transfers between devices, per_device(): lax.ppermute(skus, 'z_hi', [(i, (i + k) % 4) for i in range(4)])  13.1 us
    pallas_call x1, Pallas kernels, per_device(): kernel_call(image_kernel, shape((16, 32, 128)), 3, smem=1, name='image',...  8.85 us
  transfers between devices with their start and end apart: 4, of which 2 were waited for; matrix products, arithmetic and copies ran while one was open for 0% of the time, Pallas kernels for 0%

profile of v1, /device:TPU:1, one launch (start us, length us, event | category | flops | bytes accessed | tf_op | source)
XLA Modules:
  0.0 176.5 jit_solution(16288307642023739604)
XLA Ops:
  0.0 0.0 copy-start
  0.0 0.8 copy-done
  0.8 0.0 copy-start.1
  0.8 0.7 copy-done.1
  1.5 0.0 copy-start.2
  1.5 0.7 copy-done.2
  2.2 0.2 pack.1
  2.3 22.4 %all_to_all.30 = bf16[8,16,128]{2,1,0:T(8,128)(2,1)S(1)} all-to-all(bf16[8,16,128]{2,1,0:T(8,128)(2,1)S(1)} %get-tuple-element.14), channel_id=1, replica_groups=mesh['z_hi'=4,'core'=2,'y'=4,'x'=4,'z_lo'=8] {'z_lo'}, dimensions={0} | all-to-all | bytes 65536 | tf_op jit(solution)/shard_map/all_to_all | solution.py:129
  24.7 0.9 broadcast_in_dim.12
  25.6 6.8 %all-to-all-start.1 = ((bf16[16,128,128]{2,1,0:T(8,128)(2,1)}), bf16[16,128,128]{2,1,0:T(8,128)(2,1)S(1)}, u32[]{:S(2)}, u32[]{:S(2)}) async-start(bf16[16,128,128]{2,1,0:T(8,128)(2,1)} %broadcast_in_dim.12), calls=%async_computation.1 | async-start | bytes 1048576 | tf_op jit(solution)/shard_map/all_to_all | solution.py:131
  32.3 15.4 %collective-permute-start = (bf16[16,1280]{1,0:T(8,128)(2,1)S(1)}, bf16[16,1280]{1,0:T(8,128)(2,1)S(1)}, u32[]{:S(2)}, u32[]{:S(2)}) collective-permute-start(bf16[16,1280]{1,0:T(8,128)(2,1)S(1)} %get-tuple-element.17), channel_id=1, source_target_pairs={{0,256},{256,512},{512,768},{768,0},{1,257},{257,513},{513,769},{7... | collective-permute-start | bytes 122888 | tf_op jit(solution)/shard_map/ppermute | solution.py:127
  47.8 11.6 %collective-permute-start.1 = (bf16[16,1280]{1,0:T(8,128)(2,1)S(1)}, bf16[16,1280]{1,0:T(8,128)(2,1)S(1)}, u32[]{:S(2)}, u32[]{:S(2)}) collective-permute-start(bf16[16,1280]{1,0:T(8,128)(2,1)S(1)} %get-tuple-element.17), channel_id=1, source_target_pairs={{0,512},{256,768},{512,0},{768,256},{1,513},{257,769},{513,1},{769... | collective-permute-start | bytes 122888 | tf_op jit(solution)/shard_map/ppermute | solution.py:127
  59.4 8.2 %collective-permute-start.2 = (bf16[16,1280]{1,0:T(8,128)(2,1)S(1)}, bf16[16,1280]{1,0:T(8,128)(2,1)S(1)}, u32[]{:S(2)}, u32[]{:S(2)}) collective-permute-start(bf16[16,1280]{1,0:T(8,128)(2,1)S(1)} %get-tuple-element.17), channel_id=1, source_target_pairs={{0,768},{256,0},{512,256},{768,512},{1,769},{257,1},{513,257},{769... | collective-permute-start | bytes 122888 | tf_op jit(solution)/shard_map/ppermute | solution.py:127
  67.5 0.0 collective-permute-done
  67.5 3.9 %collective-permute-done.1 = bf16[16,1280]{1,0:T(8,128)(2,1)S(1)} collective-permute-done((bf16[16,1280]{1,0:T(8,128)(2,1)S(1)}, bf16[16,1280]{1,0:T(8,128)(2,1)S(1)}, u32[]{:S(2)}, u32[]{:S(2)}) %collective-permute-start.1) | collective-permute-done | bytes 40992 | tf_op jit(solution)/shard_map/ppermute | solution.py:127
  71.5 9.2 %collective-permute-done.2 = bf16[16,1280]{1,0:T(8,128)(2,1)S(1)} collective-permute-done((bf16[16,1280]{1,0:T(8,128)(2,1)S(1)}, bf16[16,1280]{1,0:T(8,128)(2,1)S(1)}, u32[]{:S(2)}, u32[]{:S(2)}) %collective-permute-start.2) | collective-permute-done | bytes 40992 | tf_op jit(solution)/shard_map/ppermute | solution.py:127
  80.7 0.0 all-to-all-done.1
  80.7 2.2 %all-gather = bf16[8,16,1280]{2,1,0:T(8,128)(2,1)S(1)} all-gather(bf16[4,16,1280]{2,1,0:T(8,128)(2,1)S(1)} %pad_maximum_fusion), channel_id=2, replica_groups=mesh['z_hi'=4,'core'=2,'y'=4,'x'=4,'z_lo'=8] {'core'}, dimensions={0}, use_global_device_ids=true | all-gather | bytes 491520 | tf_op jit(solution)/shard_map/all_gather | solution.py:133
  82.9 8.9 %image.1 = f32[16,32,128]{2,1,0:T(8,128)S(1)} custom-call(s32[1]{0:T(128)} %bitcast.z_hi_ref, bf16[2048,128]{1,0:T(8,128)(2,1)S(1)} %bitcast.10, bf16[2,4,16,1280]{3,2,1,0:T(8,128)(2,1)S(1)} %bitcast.11), custom_call_target="tpu_custom_call" | custom-call | tf_op jit(solution)/shard_map/image/pallas_call | solution.py:135
  91.7 14.7 %all_to_all.31.parts_ref = f32[16,32,128]{2,1,0:T(8,128)S(1)} all-to-all(f32[16,32,128]{2,1,0:T(8,128)S(1)} %image.1), channel_id=1, replica_groups=mesh['z_hi'=4,'core'=2,'y'=4,'x'=4,'z_lo'=8] {'y','x'}, dimensions={0} | all-to-all | bytes 524288 | tf_op jit(solution)/shard_map/all_to_all | solution.py:140
  106.5 0.2 turn.1
  106.7 0.0 copy-start.3
  106.7 13.3 %all_to_all.32.parts_ref = f32[8,4,128]{2,1,0:T(4,128)S(1)} all-to-all(f32[8,4,128]{2,1,0:T(4,128)S(1)} %turn.1), channel_id=1, replica_groups=mesh['z_hi'=4,'core'=2,'y'=4,'x'=4,'z_lo'=8] {'z_lo'}, dimensions={0} | all-to-all | bytes 32768 | tf_op jit(solution)/shard_map/all_to_all | solution.py:142
  120.0 0.0 copy-done.3
  120.0 0.4 gram.1
  120.4 13.4 %all_to_all.33.parts_ref = f32[32,8,128]{2,1,0:T(8,128)S(1)} all-to-all(f32[32,8,128]{2,1,0:T(8,128)S(1)} %get-tuple-element.21), channel_id=1, replica_groups=mesh['z_hi'=4,'core'=2,'y'=4,'x'=4,'z_lo'=8] {'core','y','x'}, dimensions={0} | all-to-all | bytes 262144 | tf_op jit(solution)/shard_map/all_to_all | solution.py:146
  133.9 40.7 %all_to_all.34.parts_ref = f32[32,8,128]{2,1,0:T(8,128)S(1)} all-to-all(f32[32,8,128]{2,1,0:T(8,128)S(1)} %sum.1), channel_id=1, replica_groups=mesh['z_hi'=4,'core'=2,'y'=4,'x'=4,'z_lo'=8] {'z_hi','z_lo'}, dimensions={0} | all-to-all | bytes 262144 | tf_op jit(solution)/shard_map/all_to_all | solution.py:148
  174.6 1.9 %basis.1 = f32[16,32]{1,0:T(8,128)} custom-call(f32[32,8,128]{2,1,0:T(8,128)S(1)} %all_to_all.34.parts_ref, f32[16,32]{1,0:T(8,128)S(1)} %get-tuple-element.22.image_ref), custom_call_target="tpu_custom_call" | custom-call | tf_op jit(solution)/shard_map/basis/pallas_call | solution.py:149
  (2 shorter events, 0.1 us)
Async XLA Ops:
  0.0 0.8 copy-start
  0.8 0.7 copy-start.1
  1.5 0.7 copy-start.2
  25.6 55.1 %all-to-all-start.1 = ((bf16[16,128,128]{2,1,0:T(8,128)(2,1)}), bf16[16,128,128]{2,1,0:T(8,128)(2,1)S(1)}, u32[]{:S(2)}, u32[]{:S(2)}) async-start(bf16[16,128,128]{2,1,0:T(8,128)(2,1)} %broadcast_in_dim.12), calls=%async_computation.1 | async-start | bytes 1048576 | tf_op jit(solution)/shard_map/all_to_all | solution.py:131
  32.3 35.2 %collective-permute-start = (bf16[16,1280]{1,0:T(8,128)(2,1)S(1)}, bf16[16,1280]{1,0:T(8,128)(2,1)S(1)}, u32[]{:S(2)}, u32[]{:S(2)}) collective-permute-start(bf16[16,1280]{1,0:T(8,128)(2,1)S(1)} %get-tuple-element.17), channel_id=1, source_target_pairs={{0,256},{256,512},{512,768},{768,0},{1,257},{257,513},{513,769},{7... | collective-permute-start | bytes 122888 | tf_op jit(solution)/shard_map/ppermute | solution.py:127
  47.8 23.7 %collective-permute-start.1 = (bf16[16,1280]{1,0:T(8,128)(2,1)S(1)}, bf16[16,1280]{1,0:T(8,128)(2,1)S(1)}, u32[]{:S(2)}, u32[]{:S(2)}) collective-permute-start(bf16[16,1280]{1,0:T(8,128)(2,1)S(1)} %get-tuple-element.17), channel_id=1, source_target_pairs={{0,512},{256,768},{512,0},{768,256},{1,513},{257,769},{513,1},{769... | collective-permute-start | bytes 122888 | tf_op jit(solution)/shard_map/ppermute | solution.py:127
  59.4 21.3 %collective-permute-start.2 = (bf16[16,1280]{1,0:T(8,128)(2,1)S(1)}, bf16[16,1280]{1,0:T(8,128)(2,1)S(1)}, u32[]{:S(2)}, u32[]{:S(2)}) collective-permute-start(bf16[16,1280]{1,0:T(8,128)(2,1)S(1)} %get-tuple-element.17), channel_id=1, source_target_pairs={{0,768},{256,0},{512,256},{768,512},{1,769},{257,1},{513,257},{769... | collective-permute-start | bytes 122888 | tf_op jit(solution)/shard_map/ppermute | solution.py:127
  106.7 13.3 %copy-start.3 = (f32[1,32]{1,0:T(1,128)S(1)}, f32[1,32]{1,0:T(1,128)}, u32[]{:S(2)}) copy-start(f32[1,32]{1,0:T(1,128)} %weight_ref.1) | copy-start | bytes 388

commit v2 on v1

--- a/solution.py
+++ b/solution.py
@@ -11,15 +11,14 @@
 SIZES = (4, 2, 4, 4, 8)
 ROW, COL = ("z_hi", "core"), ("y", "x", "z_lo")
 VMEM = pl.BlockSpec(memory_space=pltpu.VMEM)
-SMEM = pl.BlockSpec(memory_space=pltpu.SMEM)
 T_STEP, S_STEP = 1024, 256
 
 
-def kernel_call(body, outs, count, scratch=(), smem=0, name=None, **cost):
+def kernel_call(body, outs, count, scratch=(), name=None):
     return pl.pallas_call(
         body,
         out_shape=outs,
-        in_specs=[SMEM] * smem + [VMEM] * (count - smem),
+        in_specs=[VMEM] * count,
         out_specs=jax.tree.map(lambda _: VMEM, outs),
         scratch_shapes=list(scratch),
         name=name,
@@ -44,12 +43,10 @@
     skus_ref[...] = jnp.concatenate([factors, columns], axis=1).astype(BF16)
 
 
-def image_kernel(z_hi_ref, strips_ref, panel_ref, out_ref, wide_ref, columns_ref, unit_ref, turned_ref):
-    z_hi = z_hi_ref[0]
-    for back in range(4):
-        place = lax.rem(z_hi + 4 - back, 4)
+def image_kernel(strips_ref, panel_ref, out_ref, wide_ref, columns_ref, unit_ref, turned_ref):
+    for place in range(4):
         for core in range(2):
-            piece = panel_ref[core, back].astype(F32)
+            piece = panel_ref[core, place].astype(F32)
             wide_ref[place, core, :, :1024] = piece[:8, :1024]
             wide_ref[place, core, :, 1024:] = piece[8:, :1024]
             for m in range(8):
@@ -91,7 +88,7 @@
         image * weight_ref[...], image, (((1,), (1,)), ((), ())),
         precision=lax.Precision.HIGHEST, preferred_element_type=F32,
     )
-    packed = jnp.concatenate([gram[:8], gram[8:], jnp.zeros((8, 96), F32)], axis=1)
+    packed = jnp.concatenate([gram[2 * b : 2 * b + 2] for b in range(8)], axis=1)
     gram_ref[...] = jnp.broadcast_to(packed[None], gram_ref.shape)
 
 
@@ -106,7 +103,7 @@
     total = parts_ref[0]
     for k in range(1, parts_ref.shape[0]):
         total = total + parts_ref[k]
-    gram = jnp.concatenate([total[:, :16], total[:, 16:32]], axis=0)
+    gram = jnp.concatenate([total[:, 16 * b : 16 * b + 16] for b in range(8)], axis=0)
     left = image_ref[...]
     rows = lax.broadcasted_iota(jnp.int32, (16, 1), 0)
     for k in range(15):
@@ -121,30 +118,24 @@
 
 def per_device(strip_factors, sku_factors, probe, demand_weight):
     strips, skus = kernel_call(
-        pack_kernel, (shape((8, 16, 128), BF16), shape((16, 1280), BF16)), 3, name="pack"
+        pack_kernel, (shape((128, 16, 128), BF16), shape((16, 1280), BF16)), 3, name="pack"
     )(strip_factors, sku_factors.T, probe.T)
-    shards = [skus] + [
-        lax.ppermute(skus, "z_hi", [(i, (i + k) % 4) for i in range(4)]) for k in range(1, 4)
-    ]
-    strips = lax.all_to_all(strips, "z_lo", 0, 0, tiled=True).reshape(128, 128)
-    strips = jnp.broadcast_to(strips[None], (16, 128, 128))
-    strips = lax.all_to_all(strips, ("y", "x"), 0, 0, tiled=True).reshape(2048, 128)
-    strips, *shards = lax.optimization_barrier((strips, *shards))
-    panel = lax.all_gather(jnp.stack(shards), "core", axis=0)
-    place = jnp.full((1,), lax.axis_index("z_hi"), jnp.int32)
+    panel = lax.all_gather(skus, "z_hi", axis=0)
+    strips = lax.all_to_all(strips, COL, 0, 0, tiled=True).reshape(2048, 128)
+    panel = lax.all_gather(panel, "core", axis=0)
     total = kernel_call(
-        image_kernel, shape((16, 32, 128)), 3, smem=1, name="image",
+        image_kernel, shape((16, 32, 128)), 2, name="image",
         scratch=[pltpu.VMEM((4, 2, 8, 2048), F32), pltpu.VMEM((4, 2, 2, 2048), F32),
                  pltpu.VMEM((2048, 64), BF16), pltpu.VMEM((128, 2048), BF16)],
-    )(place, strips, panel)
+    )(strips, panel)
     total = lax.all_to_all(total, ("y", "x"), 0, 0, tiled=True)
     total = kernel_call(turn_kernel, shape((8, 4, 128)), 1, name="turn")(total)
     total = lax.all_to_all(total, "z_lo", 0, 0, tiled=True)
     image, gram = kernel_call(
-        gram_kernel, (shape((16, 32)), shape((32, 8, 128))), 2, name="gram"
+        gram_kernel, (shape((16, 32)), shape((32, 2, 128))), 2, name="gram"
     )(total, demand_weight)
     gram = lax.all_to_all(gram, ("core", "y", "x"), 0, 0, tiled=True)
-    gram = kernel_call(sum_kernel, shape((32, 8, 128)), 1, name="sum")(gram)
+    gram = kernel_call(sum_kernel, shape((32, 2, 128)), 1, name="sum")(gram)
     gram = lax.all_to_all(gram, ("z_hi", "z_lo"), 0, 0, tiled=True)
     return kernel_call(basis_kernel, shape((16, 32)), 2, name="basis")(gram, image)
 

time: 177 us -> 171 us (0.966)
  blocking collectives: 107 us -> 135 us
  starting transfers between devices: 41.9 us -> 20.4 us
  waiting for transfers between devices: 13.1 us -> 0.01 us
    all_gather x1 -> x2, blocking collectives: 2.17 us -> 40.4 us  [the longest x1 35.3 us: per_device(): panel = lax.all_gather(skus, 'z_hi', axis=0)]
    ppermute x3 -> x0, starting transfers between devices: 35.2 us -> none  [per_device(): lax.ppermute(skus, 'z_hi', [(i, (i + k) % 4) for i in range(4)])]
    all_to_all x1 -> x0, blocking collectives: 22.4 us -> none  [per_device(): strips = lax.all_to_all(strips, 'z_lo', 0, 0, tiled=True).reshape(128, 128)]
    all_to_all x1, blocking collectives: 13.3 us -> 34 us  [per_device(): total = lax.all_to_all(total, 'z_lo', 0, 0, tiled=True)]
    all_to_all x1, starting transfers between devices: 6.75 us -> 20.4 us  [per_device(): strips = lax.all_to_all(strips, COL, 0, 0, tiled=True).reshape(2048, 128)]
    ppermute x3 -> x0, waiting for transfers between devices: 13.1 us -> none  [per_device(): lax.ppermute(skus, 'z_hi', [(i, (i + k) % 4) for i in range(4)])]
    all_to_all x1, blocking collectives: 40.7 us -> 33.3 us  [per_device(): gram = lax.all_to_all(gram, ('z_hi', 'z_lo'), 0, 0, tiled=True)]
  transfers between devices with their start and end apart: 4 -> 1, of which waited for: 2 -> 0; matrix products, arithmetic and copies ran while one was open for 0% -> 0% of each run, Pallas kernels for 0% -> 0%
where the time goes in v2:
time: 171 us; the launch traced here: 170 us
  blocking collectives  135 us (79%)
  starting transfers between devices  20.4 us (12%)
  Pallas kernels  12.4 us (7%)
  local copies, waits for them, and re-layouts  2.16 us (1%)
    all_gather x1, blocking collectives, per_device(): panel = lax.all_gather(skus, 'z_hi', axis=0)  35.3 us
    all_to_all x1, blocking collectives, per_device(): total = lax.all_to_all(total, 'z_lo', 0, 0, tiled=True)  34 us
    all_to_all x1, blocking collectives, per_device(): gram = lax.all_to_all(gram, ('z_hi', 'z_lo'), 0, 0, tiled=True)  33.3 us
    all_to_all x1, starting transfers between devices, per_device(): strips = lax.all_to_all(strips, COL, 0, 0, tiled=True).reshape(2048, 128)  20.4 us
    all_to_all x1, blocking collectives, per_device(): total = lax.all_to_all(total, ('y', 'x'), 0, 0, tiled=True)  14.5 us
    all_to_all x1, blocking collectives, per_device(): gram = lax.all_to_all(gram, ('core', 'y', 'x'), 0, 0, tiled=True)  12.9 us
    pallas_call x1, Pallas kernels, per_device(): kernel_call(image_kernel, shape((16, 32, 128)), 2, name='image', scratch=...  8.8 us
    all_gather x1, blocking collectives, per_device(): panel = lax.all_gather(panel, 'core', axis=0)  5.08 us
  transfers between devices with their start and end apart: 1, of which 0 were waited for; matrix products, arithmetic and copies ran while one was open for 0% of the time, Pallas kernels for 0%

profile of v2, /device:TPU:1, one launch (start us, length us, event | category | flops | bytes accessed | tf_op | source)
XLA Modules:
  0.0 170.1 jit_solution(2191321338985978515)
XLA Ops:
  0.0 0.0 copy-start
  0.0 0.8 copy-done
  0.8 0.0 copy-start.1
  0.8 0.7 copy-done.1
  1.5 0.0 copy-start.2
  1.5 0.7 copy-done.2
  2.2 1.0 pack.1
  3.1 20.4 %all-to-all-start = ((bf16[128,16,128]{2,1,0:T(8,128)(2,1)}), bf16[128,16,128]{2,1,0:T(8,128)(2,1)S(1)}, u32[]{:S(2)}, u32[]{:S(2)}) async-start(bf16[128,16,128]{2,1,0:T(8,128)(2,1)} %get-tuple-element.9), calls=%async_computation | async-start | bytes 1048576 | tf_op jit(solution)/shard_map/all_to_all | solution.py:124
  23.5 35.3 %all-gather = bf16[64,1280]{1,0:T(8,128)(2,1)S(1)} all-gather(bf16[16,1280]{1,0:T(8,128)(2,1)S(1)} %get-tuple-element.10), channel_id=2, replica_groups=mesh['z_hi'=4,'core'=2,'y'=4,'x'=4,'z_lo'=8] {'z_hi'}, dimensions={0}, use_global_device_ids=true | all-gather | bytes 204800 | tf_op jit(solution)/shard_map/all_gather | solution.py:123
  58.9 5.1 %all-gather.1 = bf16[8,16,1280]{2,1,0:T(8,128)(2,1)S(1)} all-gather(bf16[4,16,1280]{2,1,0:T(8,128)(2,1)S(1)} %bitcast.9), channel_id=3, replica_groups=mesh['z_hi'=4,'core'=2,'y'=4,'x'=4,'z_lo'=8] {'core'}, dimensions={0}, use_global_device_ids=true | all-gather | bytes 491520 | tf_op jit(solution)/shard_map/all_gather | solution.py:125
  63.9 0.0 all-to-all-done
  63.9 8.8 %image.1 = f32[16,32,128]{2,1,0:T(8,128)S(1)} custom-call(bf16[2048,128]{1,0:T(8,128)(2,1)S(1)} %bitcast.5, bf16[2,4,16,1280]{3,2,1,0:T(8,128)(2,1)S(1)} %bitcast.6), custom_call_target="tpu_custom_call" | custom-call | tf_op jit(solution)/shard_map/image/pallas_call | solution.py:126
  72.7 14.5 %all_to_all.25.parts_ref = f32[16,32,128]{2,1,0:T(8,128)S(1)} all-to-all(f32[16,32,128]{2,1,0:T(8,128)S(1)} %image.1), channel_id=1, replica_groups=mesh['z_hi'=4,'core'=2,'y'=4,'x'=4,'z_lo'=8] {'y','x'}, dimensions={0} | all-to-all | bytes 524288 | tf_op jit(solution)/shard_map/all_to_all | solution.py:131
  87.2 0.2 turn.1
  87.4 0.0 copy-start.3
  87.5 34.0 %all_to_all.26.parts_ref = f32[8,4,128]{2,1,0:T(4,128)S(1)} all-to-all(f32[8,4,128]{2,1,0:T(4,128)S(1)} %turn.1), channel_id=1, replica_groups=mesh['z_hi'=4,'core'=2,'y'=4,'x'=4,'z_lo'=8] {'z_lo'}, dimensions={0} | all-to-all | bytes 32768 | tf_op jit(solution)/shard_map/all_to_all | solution.py:133
  121.5 0.0 copy-done.3
  121.5 0.4 gram.1
  121.9 12.9 %all_to_all.27.parts_ref = f32[32,2,128]{2,1,0:T(2,128)S(1)} all-to-all(f32[32,2,128]{2,1,0:T(2,128)S(1)} %get-tuple-element.11), channel_id=1, replica_groups=mesh['z_hi'=4,'core'=2,'y'=4,'x'=4,'z_lo'=8] {'core','y','x'}, dimensions={0} | all-to-all | bytes 65536 | tf_op jit(solution)/shard_map/all_to_all | solution.py:137
  134.9 33.3 %all_to_all.28.parts_ref = f32[32,2,128]{2,1,0:T(2,128)S(1)} all-to-all(f32[32,2,128]{2,1,0:T(2,128)S(1)} %sum.1), channel_id=1, replica_groups=mesh['z_hi'=4,'core'=2,'y'=4,'x'=4,'z_lo'=8] {'z_hi','z_lo'}, dimensions={0} | all-to-all | bytes 65536 | tf_op jit(solution)/shard_map/all_to_all | solution.py:139
  168.1 2.0 %basis.1 = f32[16,32]{1,0:T(8,128)} custom-call(f32[32,2,128]{2,1,0:T(2,128)S(1)} %all_to_all.28.parts_ref, f32[16,32]{1,0:T(8,128)S(1)} %get-tuple-element.12.image_ref), custom_call_target="tpu_custom_call" | custom-call | tf_op jit(solution)/shard_map/basis/pallas_call | solution.py:140
  (1 shorter events, 0.0 us)
Async XLA Ops:
  0.0 0.8 copy-start
  0.8 0.7 copy-start.1
  1.5 0.7 copy-start.2
  3.1 60.8 %all-to-all-start = ((bf16[128,16,128]{2,1,0:T(8,128)(2,1)}), bf16[128,16,128]{2,1,0:T(8,128)(2,1)S(1)}, u32[]{:S(2)}, u32[]{:S(2)}) async-start(bf16[128,16,128]{2,1,0:T(8,128)(2,1)} %get-tuple-element.9), calls=%async_computation | async-start | bytes 1048576 | tf_op jit(solution)/shard_map/all_to_all | solution.py:124
  87.4 34.0 %copy-start.3 = (f32[1,32]{1,0:T(1,128)S(1)}, f32[1,32]{1,0:T(1,128)}, u32[]{:S(2)}) copy-start(f32[1,32]{1,0:T(1,128)} %weight_ref.1) | copy-start | bytes 388

commit v3 on v2

--- a/solution.py
+++ b/solution.py
@@ -11,10 +11,10 @@
 SIZES = (4, 2, 4, 4, 8)
 ROW, COL = ("z_hi", "core"), ("y", "x", "z_lo")
 VMEM = pl.BlockSpec(memory_space=pltpu.VMEM)
-T_STEP, S_STEP = 1024, 256
+T_STEP, S_STEP = 1024, 512
 
 
-def kernel_call(body, outs, count, scratch=(), name=None):
+def kernel_call(body, outs, count, scratch=(), name=None, room=40):
     return pl.pallas_call(
         body,
         out_shape=outs,
@@ -22,7 +22,7 @@
         out_specs=jax.tree.map(lambda _: VMEM, outs),
         scratch_shapes=list(scratch),
         name=name,
-        compiler_params=pltpu.CompilerParams(vmem_limit_bytes=40 * 2**20),
+        compiler_params=pltpu.CompilerParams(vmem_limit_bytes=room * 2**20),
     )
 
 
@@ -43,18 +43,20 @@
     skus_ref[...] = jnp.concatenate([factors, columns], axis=1).astype(BF16)
 
 
-def image_kernel(strips_ref, panel_ref, out_ref, wide_ref, columns_ref, unit_ref, turned_ref):
-    for place in range(4):
+def prepare_kernel(panel_ref, unit_ref, probe_ref):
+    factors, columns = [], []
+    for z_hi in range(4):
         for core in range(2):
-            piece = panel_ref[core, place].astype(F32)
-            wide_ref[place, core, :, :1024] = piece[:8, :1024]
-            wide_ref[place, core, :, 1024:] = piece[8:, :1024]
-            for m in range(8):
-                columns_ref[place, core, :, 256 * m : 256 * (m + 1)] = piece[2 * m : 2 * m + 2, 1024:]
-    wide = wide_ref[...].reshape(64, 2048)
+            piece = panel_ref[core, z_hi].astype(F32)
+            factors.append(jnp.concatenate([piece[:8, :1024], piece[8:, :1024]], axis=1))
+            columns.append(jnp.concatenate([piece[2 * m : 2 * m + 2, 1024:] for m in range(8)], axis=1))
+    wide = jnp.concatenate(factors, axis=0)
     scale = lax.rsqrt(jnp.sum(wide * wide, axis=0, keepdims=True) + 1e-06)
     unit_ref[...] = (wide * scale).astype(BF16).T
-    probe = jnp.concatenate([columns_ref[r // 2, r % 2] for r in range(8)], axis=0).astype(BF16)
+    probe_ref[...] = jnp.concatenate(columns, axis=0).astype(BF16)
+
+
+def image_kernel(strips_ref, unit_ref, probe_ref, out_ref, turned_ref):
     turned_ref[...] = strips_ref[...].T
     for half in range(2):
         for step in range(2048 // T_STEP):
@@ -64,7 +66,7 @@
                 skus = slice(number * S_STEP, (number + 1) * S_STEP)
                 corr = jnp.dot(unit_ref[skus, :], strip, preferred_element_type=F32)
                 affinity = jnp.exp(corr).astype(BF16)
-                total = total + jnp.dot(probe[:, skus], affinity, preferred_element_type=F32)
+                total = total + jnp.dot(probe_ref[:, skus], affinity, preferred_element_type=F32)
             for k in range(T_STEP // 128):
                 out_ref[step * (T_STEP // 128) + k, 16 * half : 16 * half + 16, :] = total[:, 128 * k : 128 * (k + 1)]
 
@@ -118,16 +120,20 @@
 
 def per_device(strip_factors, sku_factors, probe, demand_weight):
     strips, skus = kernel_call(
-        pack_kernel, (shape((128, 16, 128), BF16), shape((16, 1280), BF16)), 3, name="pack"
+        pack_kernel, (shape((8, 16, 128), BF16), shape((16, 1280), BF16)), 3, name="pack", room=63
     )(strip_factors, sku_factors.T, probe.T)
     panel = lax.all_gather(skus, "z_hi", axis=0)
-    strips = lax.all_to_all(strips, COL, 0, 0, tiled=True).reshape(2048, 128)
+    strips = lax.all_to_all(strips, "z_lo", 0, 0, tiled=True).reshape(128, 128)
+    strips, panel = lax.optimization_barrier((strips, panel))
+    strips = jnp.broadcast_to(strips[None], (16, 128, 128))
+    strips = lax.all_to_all(strips, ("y", "x"), 0, 0, tiled=True).reshape(2048, 128)
     panel = lax.all_gather(panel, "core", axis=0)
+    unit, columns = kernel_call(
+        prepare_kernel, (shape((2048, 64), BF16), shape((16, 2048), BF16)), 1, name="prepare"
+    )(panel)
     total = kernel_call(
-        image_kernel, shape((16, 32, 128)), 2, name="image",
-        scratch=[pltpu.VMEM((4, 2, 8, 2048), F32), pltpu.VMEM((4, 2, 2, 2048), F32),
-                 pltpu.VMEM((2048, 64), BF16), pltpu.VMEM((128, 2048), BF16)],
-    )(strips, panel)
+        image_kernel, shape((16, 32, 128)), 3, name="image", scratch=[pltpu.VMEM((128, 2048), BF16)]
+    )(strips, unit, columns)
     total = lax.all_to_all(total, ("y", "x"), 0, 0, tiled=True)
     total = kernel_call(turn_kernel, shape((8, 4, 128)), 1, name="turn")(total)
     total = lax.all_to_all(total, "z_lo", 0, 0, tiled=True)

time: 171 us -> 158 us (0.924)
  blocking collectives: 135 us -> 122 us
  waiting for transfers between devices: 0.01 us -> 3.08 us
    all_to_all x1, blocking collectives: 34 us -> 23.4 us  [per_device(): total = lax.all_to_all(total, 'z_lo', 0, 0, tiled=True)]
    all_to_all x1, blocking collectives: 14.5 us -> 11.2 us  [per_device(): total = lax.all_to_all(total, ('y', 'x'), 0, 0, tiled=True)]
    all_to_all x1 -> x2, waiting for transfers between devices: 0.01 us -> 3.08 us  [the longest x1 3.08 us: per_device(): lax.all_to_all(strips, ('y', 'x'), 0, 0, tiled=True).reshape(2048, 128)]
    unnamed x8 -> x4, local copies, waits for them, and re-layouts: 2.16 us -> 0.01 us
    pallas_call x2 -> x3, Pallas kernels: 9.78 us -> 8.51 us  [the longest x1 6.76 us: per_device(): kernel_call(image_kernel, shape((16, 32, 128)), 3, name='image', scratch=...]
    all_to_all x1 -> x2, starting transfers between devices: 20.4 us -> 20 us  [the longest x1 13.2 us: per_device(): strips = lax.all_to_all(strips, 'z_lo', 0, 0, tiled=True).reshape(128, 128)]
  transfers between devices with their start and end apart: 1 -> 2, of which waited for: 0 -> 1; matrix products, arithmetic and copies ran while one was open for 0% -> 0% of each run, Pallas kernels for 0% -> 0%
where the time goes in v3:
time: 158 us; the launch traced here: 157 us
  blocking collectives  122 us (77%)
  starting transfers between devices  20 us (13%)
  Pallas kernels  11.2 us (7%)
  waiting for transfers between devices  3.08 us (2%)
    all_gather x1, blocking collectives, per_device(): panel = lax.all_gather(skus, 'z_hi', axis=0)  34.5 us
    all_to_all x1, blocking collectives, per_device(): gram = lax.all_to_all(gram, ('z_hi', 'z_lo'), 0, 0, tiled=True)  32.9 us
    all_to_all x1, blocking collectives, per_device(): total = lax.all_to_all(total, 'z_lo', 0, 0, tiled=True)  23.4 us
    all_to_all x1, blocking collectives, per_device(): gram = lax.all_to_all(gram, ('core', 'y', 'x'), 0, 0, tiled=True)  14.4 us
    all_to_all x1, starting transfers between devices, per_device(): strips = lax.all_to_all(strips, 'z_lo', 0, 0, tiled=True).reshape(128, 128)  13.2 us
    all_to_all x1, blocking collectives, per_device(): total = lax.all_to_all(total, ('y', 'x'), 0, 0, tiled=True)  11.2 us
    pallas_call x1, Pallas kernels, per_device(): kernel_call(image_kernel, shape((16, 32, 128)), 3, name='image', scratch=...  6.76 us
    all_to_all x1, starting transfers between devices, per_device(): lax.all_to_all(strips, ('y', 'x'), 0, 0, tiled=True).reshape(2048, 128)  6.75 us
  transfers between devices with their start and end apart: 2, of which 1 were waited for; matrix products, arithmetic and copies ran while one was open for 0% of the time, Pallas kernels for 0%

profile of v3, /device:TPU:1, one launch (start us, length us, event | category | flops | bytes accessed | tf_op | source)
XLA Modules:
  0.0 157.3 jit_solution(15193552669799603365)
XLA Ops:
  0.0 1.5 pack.1
  1.5 0.0 copy-start.1
  1.5 13.2 %all-to-all-start = ((bf16[8,16,128]{2,1,0:T(8,128)(2,1)}), bf16[8,16,128]{2,1,0:T(8,128)(2,1)S(1)}, u32[]{:S(2)}, u32[]{:S(2)}) async-start(bf16[8,16,128]{2,1,0:T(8,128)(2,1)} %get-tuple-element.13), calls=%async_computation | async-start | bytes 65536 | tf_op jit(solution)/shard_map/all_to_all | solution.py:126
  14.7 0.0 copy-done.1
  14.7 34.5 %all-gather = bf16[64,1280]{1,0:T(8,128)(2,1)S(1)} all-gather(bf16[16,1280]{1,0:T(8,128)(2,1)S(1)} %copy-done.1), channel_id=2, replica_groups=mesh['z_hi'=4,'core'=2,'y'=4,'x'=4,'z_lo'=8] {'z_hi'}, dimensions={0}, use_global_device_ids=true | all-gather | bytes 204800 | tf_op jit(solution)/shard_map/all_gather | solution.py:125
  49.2 0.0 all-to-all-done
  49.2 0.9 broadcast_in_dim.2
  50.2 6.8 %all-to-all-start.1 = ((bf16[16,128,128]{2,1,0:T(8,128)(2,1)}), bf16[16,128,128]{2,1,0:T(8,128)(2,1)S(1)}, u32[]{:S(2)}, u32[]{:S(2)}) async-start(bf16[16,128,128]{2,1,0:T(8,128)(2,1)} %broadcast_in_dim.2), calls=%async_computation.1 | async-start | bytes 1048576 | tf_op jit(solution)/shard_map/all_to_all | solution.py:129
  56.9 5.7 %all-gather.1 = bf16[8,16,1280]{2,1,0:T(8,128)(2,1)S(1)} all-gather(bf16[4,16,1280]{2,1,0:T(8,128)(2,1)S(1)} %bitcast.8), channel_id=3, replica_groups=mesh['z_hi'=4,'core'=2,'y'=4,'x'=4,'z_lo'=8] {'core'}, dimensions={0}, use_global_device_ids=true | all-gather | bytes 491520 | tf_op jit(solution)/shard_map/all_gather | solution.py:130
  62.7 0.2 prepare.1
  62.9 3.1 %all-to-all-done.1 = bf16[16,128,128]{2,1,0:T(8,128)(2,1)S(1)} async-done(((bf16[16,128,128]{2,1,0:T(8,128)(2,1)}), bf16[16,128,128]{2,1,0:T(8,128)(2,1)S(1)}, u32[]{:S(2)}, u32[]{:S(2)}) %all-to-all-start.1) | async-done | bytes 524320 | tf_op jit(solution)/shard_map/all_to_all | solution.py:129
  66.0 6.8 %image.1 = f32[16,32,128]{2,1,0:T(8,128)S(1)} custom-call(bf16[2048,128]{1,0:T(8,128)(2,1)S(1)} %bitcast.6, bf16[2048,64]{1,0:T(8,128)(2,1)S(1)} %get-tuple-element.17.unit_ref, bf16[16,2048]{1,0:T(8,128)(2,1)S(1)} %get-tuple-element.18.probe_ref), custom_call_target="tpu_custom_call" | custom-call | tf_op jit(solution)/shard_map/image/pallas_call | solution.py:134
  72.7 11.2 %all_to_all.30.parts_ref = f32[16,32,128]{2,1,0:T(8,128)S(1)} all-to-all(f32[16,32,128]{2,1,0:T(8,128)S(1)} %image.1), channel_id=1, replica_groups=mesh['z_hi'=4,'core'=2,'y'=4,'x'=4,'z_lo'=8] {'y','x'}, dimensions={0} | all-to-all | bytes 524288 | tf_op jit(solution)/shard_map/all_to_all | solution.py:137
  83.9 0.2 turn.1
  84.1 0.0 copy-start
  84.2 23.4 %all_to_all.31.parts_ref = f32[8,4,128]{2,1,0:T(4,128)S(1)} all-to-all(f32[8,4,128]{2,1,0:T(4,128)S(1)} %turn.1), channel_id=1, replica_groups=mesh['z_hi'=4,'core'=2,'y'=4,'x'=4,'z_lo'=8] {'z_lo'}, dimensions={0} | all-to-all | bytes 32768 | tf_op jit(solution)/shard_map/all_to_all | solution.py:139
  107.5 0.0 copy-done
  107.5 0.4 gram.1
  108.0 14.4 %all_to_all.32.parts_ref = f32[32,2,128]{2,1,0:T(2,128)S(1)} all-to-all(f32[32,2,128]{2,1,0:T(2,128)S(1)} %get-tuple-element.19), channel_id=1, replica_groups=mesh['z_hi'=4,'core'=2,'y'=4,'x'=4,'z_lo'=8] {'core','y','x'}, dimensions={0} | all-to-all | bytes 65536 | tf_op jit(solution)/shard_map/all_to_all | solution.py:143
  122.4 32.9 %all_to_all.33.parts_ref = f32[32,2,128]{2,1,0:T(2,128)S(1)} all-to-all(f32[32,2,128]{2,1,0:T(2,128)S(1)} %sum.1), channel_id=1, replica_groups=mesh['z_hi'=4,'core'=2,'y'=4,'x'=4,'z_lo'=8] {'z_hi','z_lo'}, dimensions={0} | all-to-all | bytes 65536 | tf_op jit(solution)/shard_map/all_to_all | solution.py:145
  155.3 2.0 %basis.1 = f32[16,32]{1,0:T(8,128)} custom-call(f32[32,2,128]{2,1,0:T(2,128)S(1)} %all_to_all.33.parts_ref, f32[16,32]{1,0:T(8,128)S(1)} %get-tuple-element.20.image_ref), custom_call_target="tpu_custom_call" | custom-call | tf_op jit(solution)/shard_map/basis/pallas_call | solution.py:146
  (1 shorter events, 0.0 us)
Async XLA Ops:
  1.5 13.2 %copy-start.1 = (bf16[16,1280]{1,0:T(8,128)(2,1)S(1)}, bf16[16,1280]{1,0:T(8,128)(2,1)}, u32[]{:S(2)}) copy-start(bf16[16,1280]{1,0:T(8,128)(2,1)} %get-tuple-element.14) | copy-start | bytes 122884
  1.5 47.7 %all-to-all-start = ((bf16[8,16,128]{2,1,0:T(8,128)(2,1)}), bf16[8,16,128]{2,1,0:T(8,128)(2,1)S(1)}, u32[]{:S(2)}, u32[]{:S(2)}) async-start(bf16[8,16,128]{2,1,0:T(8,128)(2,1)} %get-tuple-element.13), calls=%async_computation | async-start | bytes 65536 | tf_op jit(solution)/shard_map/all_to_all | solution.py:126
  50.2 15.8 %all-to-all-start.1 = ((bf16[16,128,128]{2,1,0:T(8,128)(2,1)}), bf16[16,128,128]{2,1,0:T(8,128)(2,1)S(1)}, u32[]{:S(2)}, u32[]{:S(2)}) async-start(bf16[16,128,128]{2,1,0:T(8,128)(2,1)} %broadcast_in_dim.2), calls=%async_computation.1 | async-start | bytes 1048576 | tf_op jit(solution)/shard_map/all_to_all | solution.py:129
  84.1 23.4 %copy-start = (f32[1,32]{1,0:T(1,128)S(1)}, f32[1,32]{1,0:T(1,128)}, u32[]{:S(2)}) copy-start(f32[1,32]{1,0:T(1,128)} %weight_ref.1) | copy-start | bytes 388

commit v4 on v3

--- a/solution.py
+++ b/solution.py
@@ -118,13 +118,17 @@
     out_ref[...] = left / jnp.sqrt(pivots)
 
 
+def from_first(pieces, axes, first):
+    others = [k for k in range(pieces.shape[0]) if k != first]
+    return lax.all_to_all(pieces, axes, 0, 0, axis_index_groups=[[first, *others]], tiled=True)
+
+
 def per_device(strip_factors, sku_factors, probe, demand_weight):
     strips, skus = kernel_call(
         pack_kernel, (shape((8, 16, 128), BF16), shape((16, 1280), BF16)), 3, name="pack", room=63
     )(strip_factors, sku_factors.T, probe.T)
     panel = lax.all_gather(skus, "z_hi", axis=0)
-    strips = lax.all_to_all(strips, "z_lo", 0, 0, tiled=True).reshape(128, 128)
-    strips, panel = lax.optimization_barrier((strips, panel))
+    strips = from_first(strips, "z_lo", 3).reshape(128, 128)
     strips = jnp.broadcast_to(strips[None], (16, 128, 128))
     strips = lax.all_to_all(strips, ("y", "x"), 0, 0, tiled=True).reshape(2048, 128)
     panel = lax.all_gather(panel, "core", axis=0)
@@ -136,13 +140,13 @@
     )(strips, unit, columns)
     total = lax.all_to_all(total, ("y", "x"), 0, 0, tiled=True)
     total = kernel_call(turn_kernel, shape((8, 4, 128)), 1, name="turn")(total)
-    total = lax.all_to_all(total, "z_lo", 0, 0, tiled=True)
+    total = from_first(total, "z_lo", 3)
     image, gram = kernel_call(
         gram_kernel, (shape((16, 32)), shape((32, 2, 128))), 2, name="gram"
     )(total, demand_weight)
     gram = lax.all_to_all(gram, ("core", "y", "x"), 0, 0, tiled=True)
     gram = kernel_call(sum_kernel, shape((32, 2, 128)), 1, name="sum")(gram)
-    gram = lax.all_to_all(gram, ("z_hi", "z_lo"), 0, 0, tiled=True)
+    gram = from_first(gram, ("z_hi", "z_lo"), 16)
     return kernel_call(basis_kernel, shape((16, 32)), 2, name="basis")(gram, image)
 
 

time: 158 us -> 146 us (0.924)
  starting transfers between devices: 20 us -> 6.89 us
  blocking collectives: 122 us -> 126 us
  waiting for transfers between devices: 3.08 us -> 0.01 us
    all_to_all x1 -> x0, starting transfers between devices: 13.2 us -> none  [per_device(): strips = lax.all_to_all(strips, 'z_lo', 0, 0, tiled=True).reshape(128, 128)]
    all_to_all x1, blocking collectives: 11.2 us -> 16.6 us  [per_device(): total = lax.all_to_all(total, ('y', 'x'), 0, 0, tiled=True)]
    all_to_all x1, waiting for transfers between devices: 3.08 us -> 0.01 us  [per_device(): lax.all_to_all(strips, ('y', 'x'), 0, 0, tiled=True).reshape(2048, 128)]
    all_to_all x2 -> x3, blocking collectives: 56.2 us -> 54.6 us  [from_first(): lax.all_to_all(pieces, axes, 0, 0, axis_index_groups=[[first, *others]],...]
  transfers between devices with their start and end apart: 2 -> 1, of which waited for: 1 -> 0; matrix products, arithmetic and copies ran while one was open for 0% -> 0% of each run, Pallas kernels for 0% -> 0%
where the time goes in v4:
time: 146 us; the launch traced here: 145 us
  blocking collectives  126 us (86%)
  Pallas kernels  11.2 us (8%)
  starting transfers between devices  6.89 us (5%)
    all_to_all x3, blocking collectives, from_first(): lax.all_to_all(pieces, axes, 0, 0, axis_index_groups=[[first, *others]],...  54.6 us
    all_gather x1, blocking collectives, per_device(): panel = lax.all_gather(skus, 'z_hi', axis=0)  35.4 us
    all_to_all x1, blocking collectives, per_device(): total = lax.all_to_all(total, ('y', 'x'), 0, 0, tiled=True)  16.6 us
    all_to_all x1, blocking collectives, per_device(): gram = lax.all_to_all(gram, ('core', 'y', 'x'), 0, 0, tiled=True)  12.9 us
    all_to_all x1, starting transfers between devices, per_device(): lax.all_to_all(strips, ('y', 'x'), 0, 0, tiled=True).reshape(2048, 128)  6.89 us
    pallas_call x1, Pallas kernels, per_device(): kernel_call(image_kernel, shape((16, 32, 128)), 3, name='image', scratch=...  6.76 us
    all_gather x1, blocking collectives, per_device(): panel = lax.all_gather(panel, 'core', axis=0)  6.47 us
  transfers between devices with their start and end apart: 1, of which 0 were waited for; matrix products, arithmetic and copies ran while one was open for 0% of the time, Pallas kernels for 0%

profile of v4, /device:TPU:1, one launch (start us, length us, event | category | flops | bytes accessed | tf_op | source)
XLA Modules:
  0.0 145.0 jit_solution(13927205468019093572)
XLA Ops:
  0.0 1.5 %pack.1 = (bf16[8,16,128]{2,1,0:T(8,128)(2,1)}, bf16[16,1280]{1,0:T(8,128)(2,1)}) custom-call(bf16[32,64]{1,0:T(8,128)(2,1)} %strip_ref.1, bf16[8,2048]{1,0:T(8,128)(2,1)} %bitcast.10, bf16[2,2048]{1,0:T(2,128)(2,1)} %bitcast.11), custom_call_target="tpu_custom_call" | custom-call | tf_op jit(solution)/shard_map/pack/pallas_call | solution.py:127
  1.5 19.8 %all_to_all.30 = bf16[8,16,128]{2,1,0:T(8,128)(2,1)S(1)} all-to-all(bf16[8,16,128]{2,1,0:T(8,128)(2,1)} %get-tuple-element.11), channel_id=1, replica_groups={{3,0,1,2,4,5,6,7},{11,8,9,10,12,13,14,15},{19,16,17,18,20,21,22,23},{27..., dimensions={0} | all-to-all | bytes 65536 | tf_op jit(solution)/shard_map/all_to_all | solution.py:123
  21.3 0.9 broadcast_in_dim.8
  22.2 0.0 copy-start.1
  22.2 6.9 %all-to-all-start.1 = ((bf16[16,128,128]{2,1,0:T(8,128)(2,1)}), bf16[16,128,128]{2,1,0:T(8,128)(2,1)S(1)}, u32[]{:S(2)}, u32[]{:S(2)}) async-start(bf16[16,128,128]{2,1,0:T(8,128)(2,1)} %broadcast_in_dim.8), calls=%async_computation.1 | async-start | bytes 1048576 | tf_op jit(solution)/shard_map/all_to_all | solution.py:133
  29.1 0.0 copy-done.1
  29.1 35.4 %all-gather = bf16[64,1280]{1,0:T(8,128)(2,1)S(1)} all-gather(bf16[16,1280]{1,0:T(8,128)(2,1)S(1)} %copy-done.1), channel_id=2, replica_groups=mesh['z_hi'=4,'core'=2,'y'=4,'x'=4,'z_lo'=8] {'z_hi'}, dimensions={0}, use_global_device_ids=true | all-gather | bytes 204800 | tf_op jit(solution)/shard_map/all_gather | solution.py:130
  64.5 6.5 %all-gather.1 = bf16[8,16,1280]{2,1,0:T(8,128)(2,1)S(1)} all-gather(bf16[4,16,1280]{2,1,0:T(8,128)(2,1)S(1)} %bitcast.8), channel_id=3, replica_groups=mesh['z_hi'=4,'core'=2,'y'=4,'x'=4,'z_lo'=8] {'core'}, dimensions={0}, use_global_device_ids=true | all-gather | bytes 491520 | tf_op jit(solution)/shard_map/all_gather | solution.py:134
  71.0 0.2 prepare.1
  71.2 0.0 all-to-all-done.1
  71.2 6.8 %image.1 = f32[16,32,128]{2,1,0:T(8,128)S(1)} custom-call(bf16[2048,128]{1,0:T(8,128)(2,1)S(1)} %bitcast.6, bf16[2048,64]{1,0:T(8,128)(2,1)S(1)} %get-tuple-element.13.unit_ref, bf16[16,2048]{1,0:T(8,128)(2,1)S(1)} %get-tuple-element.14.probe_ref), custom_call_target="tpu_custom_call" | custom-call | tf_op jit(solution)/shard_map/image/pallas_call | solution.py:138
  78.0 16.6 %all_to_all.31.parts_ref = f32[16,32,128]{2,1,0:T(8,128)S(1)} all-to-all(f32[16,32,128]{2,1,0:T(8,128)S(1)} %image.1), channel_id=1, replica_groups=mesh['z_hi'=4,'core'=2,'y'=4,'x'=4,'z_lo'=8] {'y','x'}, dimensions={0} | all-to-all | bytes 524288 | tf_op jit(solution)/shard_map/all_to_all | solution.py:141
  94.6 0.2 turn.1
  94.8 0.0 copy-start
  94.8 10.7 %all_to_all.32.parts_ref = f32[8,4,128]{2,1,0:T(4,128)S(1)} all-to-all(f32[8,4,128]{2,1,0:T(4,128)S(1)} %turn.1), channel_id=1, replica_groups={{3,0,1,2,4,5,6,7},{11,8,9,10,12,13,14,15},{19,16,17,18,20,21,22,23},{27..., dimensions={0} | all-to-all | bytes 32768 | tf_op jit(solution)/shard_map/all_to_all | solution.py:123
  105.4 0.0 copy-done
  105.4 0.4 gram.1
  105.9 12.9 %all_to_all.33.parts_ref = f32[32,2,128]{2,1,0:T(2,128)S(1)} all-to-all(f32[32,2,128]{2,1,0:T(2,128)S(1)} %get-tuple-element.15), channel_id=1, replica_groups=mesh['z_hi'=4,'core'=2,'y'=4,'x'=4,'z_lo'=8] {'core','y','x'}, dimensions={0} | all-to-all | bytes 65536 | tf_op jit(solution)/shard_map/all_to_all | solution.py:147
  118.8 24.2 %all_to_all.34.parts_ref = f32[32,2,128]{2,1,0:T(2,128)S(1)} all-to-all(f32[32,2,128]{2,1,0:T(2,128)S(1)} %sum.1), channel_id=1, replica_groups={{512,0,1,2,3,4,5,6,7,256,257,258,259,260,261,262,263,513,514,515,516,51..., dimensions={0} | all-to-all | bytes 65536 | tf_op jit(solution)/shard_map/all_to_all | solution.py:123
  143.0 2.0 %basis.1 = f32[16,32]{1,0:T(8,128)} custom-call(f32[32,2,128]{2,1,0:T(2,128)S(1)} %all_to_all.34.parts_ref, f32[16,32]{1,0:T(8,128)S(1)} %get-tuple-element.16.image_ref), custom_call_target="tpu_custom_call" | custom-call | tf_op jit(solution)/shard_map/basis/pallas_call | solution.py:150
  (1 shorter events, 0.0 us)
Async XLA Ops:
  22.2 6.9 %copy-start.1 = (bf16[16,1280]{1,0:T(8,128)(2,1)S(1)}, bf16[16,1280]{1,0:T(8,128)(2,1)}, u32[]{:S(2)}) copy-start(bf16[16,1280]{1,0:T(8,128)(2,1)} %get-tuple-element.12) | copy-start | bytes 122884
  22.2 49.0 %all-to-all-start.1 = ((bf16[16,128,128]{2,1,0:T(8,128)(2,1)}), bf16[16,128,128]{2,1,0:T(8,128)(2,1)S(1)}, u32[]{:S(2)}, u32[]{:S(2)}) async-start(bf16[16,128,128]{2,1,0:T(8,128)(2,1)} %broadcast_in_dim.8), calls=%async_computation.1 | async-start | bytes 1048576 | tf_op jit(solution)/shard_map/all_to_all | solution.py:133
  94.8 10.7 %copy-start = (f32[1,32]{1,0:T(1,128)S(1)}, f32[1,32]{1,0:T(1,128)}, u32[]{:S(2)}) copy-start(f32[1,32]{1,0:T(1,128)} %weight_ref.1) | copy-start | bytes 388

commit v5 on v4

--- a/solution.py
+++ b/solution.py
@@ -128,7 +128,8 @@
         pack_kernel, (shape((8, 16, 128), BF16), shape((16, 1280), BF16)), 3, name="pack", room=63
     )(strip_factors, sku_factors.T, probe.T)
     panel = lax.all_gather(skus, "z_hi", axis=0)
-    strips = from_first(strips, "z_lo", 3).reshape(128, 128)
+    strips = from_first(strips, "z_lo", 4).reshape(128, 128)
+    strips, panel = lax.optimization_barrier((strips, panel))
     strips = jnp.broadcast_to(strips[None], (16, 128, 128))
     strips = lax.all_to_all(strips, ("y", "x"), 0, 0, tiled=True).reshape(2048, 128)
     panel = lax.all_gather(panel, "core", axis=0)
@@ -140,7 +141,7 @@
     )(strips, unit, columns)
     total = lax.all_to_all(total, ("y", "x"), 0, 0, tiled=True)
     total = kernel_call(turn_kernel, shape((8, 4, 128)), 1, name="turn")(total)
-    total = from_first(total, "z_lo", 3)
+    total = from_first(total, "z_lo", 4)
     image, gram = kernel_call(
         gram_kernel, (shape((16, 32)), shape((32, 2, 128))), 2, name="gram"
     )(total, demand_weight)

time: 146 us -> 142 us (0.973)
  blocking collectives: 126 us -> 107 us
  starting transfers between devices: 6.89 us -> 20.2 us
  waiting for transfers between devices: 0.01 us -> 1.88 us
    all_to_all x3 -> x2, blocking collectives: 54.6 us -> 34.9 us  [from_first(): lax.all_to_all(pieces, axes, 0, 0, axis_index_groups=[[first, *others]],...]
    all_to_all x0 -> x1, starting transfers between devices: none -> 13.5 us  [from_first(): lax.all_to_all(pieces, axes, 0, 0, axis_index_groups=[[first, *others]],...]
    all_to_all x1, blocking collectives: 16.6 us -> 12.4 us  [per_device(): total = lax.all_to_all(total, ('y', 'x'), 0, 0, tiled=True)]
    all_to_all x1, blocking collectives: 12.9 us -> 17 us  [per_device(): gram = lax.all_to_all(gram, ('core', 'y', 'x'), 0, 0, tiled=True)]
    all_to_all x1, waiting for transfers between devices: 0.01 us -> 1.88 us  [per_device(): lax.all_to_all(strips, ('y', 'x'), 0, 0, tiled=True).reshape(2048, 128)]
  transfers between devices with their start and end apart: 1 -> 2, of which waited for: 0 -> 1; matrix products, arithmetic and copies ran while one was open for 0% -> 0% of each run, Pallas kernels for 0% -> 0%
where the time goes in v5:
time: 142 us
  blocking collectives  107 us (75%)
  starting transfers between devices  20.2 us (14%)
  Pallas kernels  11.2 us (8%)
  waiting for transfers between devices  1.88 us (1%)
    all_gather x1, blocking collectives, per_device(): panel = lax.all_gather(skus, 'z_hi', axis=0)  36.2 us
    all_to_all x2, blocking collectives, from_first(): lax.all_to_all(pieces, axes, 0, 0, axis_index_groups=[[first, *others]],...  34.9 us
    all_to_all x1, blocking collectives, per_device(): gram = lax.all_to_all(gram, ('core', 'y', 'x'), 0, 0, tiled=True)  17 us
    all_to_all x1, starting transfers between devices, from_first(): lax.all_to_all(pieces, axes, 0, 0, axis_index_groups=[[first, *others]],...  13.5 us
    all_to_all x1, blocking collectives, per_device(): total = lax.all_to_all(total, ('y', 'x'), 0, 0, tiled=True)  12.4 us
    all_gather x1, blocking collectives, per_device(): panel = lax.all_gather(panel, 'core', axis=0)  6.87 us
    pallas_call x1, Pallas kernels, per_device(): kernel_call(image_kernel, shape((16, 32, 128)), 3, name='image', scratch=...  6.76 us
    all_to_all x1, starting transfers between devices, per_device(): lax.all_to_all(strips, ('y', 'x'), 0, 0, tiled=True).reshape(2048, 128)  6.75 us
  transfers between devices with their start and end apart: 2, of which 1 were waited for; matrix products, arithmetic and copies ran while one was open for 0% of the time, Pallas kernels for 0%

profile of v5, /device:TPU:1, one launch (start us, length us, event | category | flops | bytes accessed | tf_op | source)
XLA Modules:
  0.0 141.6 jit_solution(4237880632302176198)
XLA Ops:
  0.0 1.5 %pack.1 = (bf16[8,16,128]{2,1,0:T(8,128)(2,1)}, bf16[16,1280]{1,0:T(8,128)(2,1)}) custom-call(bf16[32,64]{1,0:T(8,128)(2,1)} %strip_ref.1, bf16[8,2048]{1,0:T(8,128)(2,1)} %bitcast.10, bf16[2,2048]{1,0:T(2,128)(2,1)} %bitcast.11), custom_call_target="tpu_custom_call" | custom-call | tf_op jit(solution)/shard_map/pack/pallas_call | solution.py:127
  1.5 0.0 copy-start.1
  1.5 13.5 %all-to-all-start = ((bf16[8,16,128]{2,1,0:T(8,128)(2,1)}), bf16[8,16,128]{2,1,0:T(8,128)(2,1)S(1)}, u32[]{:S(2)}, u32[]{:S(2)}) async-start(bf16[8,16,128]{2,1,0:T(8,128)(2,1)} %get-tuple-element.13), calls=%async_computation | async-start | bytes 65536 | tf_op jit(solution)/shard_map/all_to_all | solution.py:123
  15.0 0.0 copy-done.1
  15.0 36.2 %all-gather = bf16[64,1280]{1,0:T(8,128)(2,1)S(1)} all-gather(bf16[16,1280]{1,0:T(8,128)(2,1)S(1)} %copy-done.1), channel_id=2, replica_groups=mesh['z_hi'=4,'core'=2,'y'=4,'x'=4,'z_lo'=8] {'z_hi'}, dimensions={0}, use_global_device_ids=true | all-gather | bytes 204800 | tf_op jit(solution)/shard_map/all_gather | solution.py:130
  51.2 0.0 all-to-all-done
  51.2 0.9 broadcast_in_dim.2
  52.2 6.8 %all-to-all-start.1 = ((bf16[16,128,128]{2,1,0:T(8,128)(2,1)}), bf16[16,128,128]{2,1,0:T(8,128)(2,1)S(1)}, u32[]{:S(2)}, u32[]{:S(2)}) async-start(bf16[16,128,128]{2,1,0:T(8,128)(2,1)} %broadcast_in_dim.2), calls=%async_computation.1 | async-start | bytes 1048576 | tf_op jit(solution)/shard_map/all_to_all | solution.py:134
  58.9 6.9 %all-gather.1 = bf16[8,16,1280]{2,1,0:T(8,128)(2,1)S(1)} all-gather(bf16[4,16,1280]{2,1,0:T(8,128)(2,1)S(1)} %bitcast.8), channel_id=3, replica_groups=mesh['z_hi'=4,'core'=2,'y'=4,'x'=4,'z_lo'=8] {'core'}, dimensions={0}, use_global_device_ids=true | all-gather | bytes 491520 | tf_op jit(solution)/shard_map/all_gather | solution.py:135
  65.8 0.2 prepare.1
  66.0 1.9 %all-to-all-done.1 = bf16[16,128,128]{2,1,0:T(8,128)(2,1)S(1)} async-done(((bf16[16,128,128]{2,1,0:T(8,128)(2,1)}), bf16[16,128,128]{2,1,0:T(8,128)(2,1)S(1)}, u32[]{:S(2)}, u32[]{:S(2)}) %all-to-all-start.1) | async-done | bytes 524320 | tf_op jit(solution)/shard_map/all_to_all | solution.py:134
  67.9 6.8 %image.1 = f32[16,32,128]{2,1,0:T(8,128)S(1)} custom-call(bf16[2048,128]{1,0:T(8,128)(2,1)S(1)} %bitcast.6, bf16[2048,64]{1,0:T(8,128)(2,1)S(1)} %get-tuple-element.17.unit_ref, bf16[16,2048]{1,0:T(8,128)(2,1)S(1)} %get-tuple-element.18.probe_ref), custom_call_target="tpu_custom_call" | custom-call | tf_op jit(solution)/shard_map/image/pallas_call | solution.py:139
  74.7 12.4 %all_to_all.30.parts_ref = f32[16,32,128]{2,1,0:T(8,128)S(1)} all-to-all(f32[16,32,128]{2,1,0:T(8,128)S(1)} %image.1), channel_id=1, replica_groups=mesh['z_hi'=4,'core'=2,'y'=4,'x'=4,'z_lo'=8] {'y','x'}, dimensions={0} | all-to-all | bytes 524288 | tf_op jit(solution)/shard_map/all_to_all | solution.py:142
  87.1 0.2 turn.1
  87.3 0.0 copy-start
  87.3 10.7 %all_to_all.31.parts_ref = f32[8,4,128]{2,1,0:T(4,128)S(1)} all-to-all(f32[8,4,128]{2,1,0:T(4,128)S(1)} %turn.1), channel_id=1, replica_groups={{4,0,1,2,3,5,6,7},{12,8,9,10,11,13,14,15},{20,16,17,18,19,21,22,23},{28..., dimensions={0} | all-to-all | bytes 32768 | tf_op jit(solution)/shard_map/all_to_all | solution.py:123
  97.9 0.0 copy-done
  98.0 0.4 gram.1
  98.4 17.0 %all_to_all.32.parts_ref = f32[32,2,128]{2,1,0:T(2,128)S(1)} all-to-all(f32[32,2,128]{2,1,0:T(2,128)S(1)} %get-tuple-element.19), channel_id=1, replica_groups=mesh['z_hi'=4,'core'=2,'y'=4,'x'=4,'z_lo'=8] {'core','y','x'}, dimensions={0} | all-to-all | bytes 65536 | tf_op jit(solution)/shard_map/all_to_all | solution.py:148
  115.4 24.2 %all_to_all.33.parts_ref = f32[32,2,128]{2,1,0:T(2,128)S(1)} all-to-all(f32[32,2,128]{2,1,0:T(2,128)S(1)} %sum.1), channel_id=1, replica_groups={{512,0,1,2,3,4,5,6,7,256,257,258,259,260,261,262,263,513,514,515,516,51..., dimensions={0} | all-to-all | bytes 65536 | tf_op jit(solution)/shard_map/all_to_all | solution.py:123
  139.6 2.0 %basis.1 = f32[16,32]{1,0:T(8,128)} custom-call(f32[32,2,128]{2,1,0:T(2,128)S(1)} %all_to_all.33.parts_ref, f32[16,32]{1,0:T(8,128)S(1)} %get-tuple-element.20.image_ref), custom_call_target="tpu_custom_call" | custom-call | tf_op jit(solution)/shard_map/basis/pallas_call | solution.py:151
  (1 shorter events, 0.0 us)
Async XLA Ops:
  1.5 13.5 %copy-start.1 = (bf16[16,1280]{1,0:T(8,128)(2,1)S(1)}, bf16[16,1280]{1,0:T(8,128)(2,1)}, u32[]{:S(2)}) copy-start(bf16[16,1280]{1,0:T(8,128)(2,1)} %get-tuple-element.14) | copy-start | bytes 122884
  1.5 49.7 %all-to-all-start = ((bf16[8,16,128]{2,1,0:T(8,128)(2,1)}), bf16[8,16,128]{2,1,0:T(8,128)(2,1)S(1)}, u32[]{:S(2)}, u32[]{:S(2)}) async-start(bf16[8,16,128]{2,1,0:T(8,128)(2,1)} %get-tuple-element.13), calls=%async_computation | async-start | bytes 65536 | tf_op jit(solution)/shard_map/all_to_all | solution.py:123
  52.2 15.8 %all-to-all-start.1 = ((bf16[16,128,128]{2,1,0:T(8,128)(2,1)}), bf16[16,128,128]{2,1,0:T(8,128)(2,1)S(1)}, u32[]{:S(2)}, u32[]{:S(2)}) async-start(bf16[16,128,128]{2,1,0:T(8,128)(2,1)} %broadcast_in_dim.2), calls=%async_computation.1 | async-start | bytes 1048576 | tf_op jit(solution)/shard_map/all_to_all | solution.py:134
  87.3 10.7 %copy-start = (f32[1,32]{1,0:T(1,128)S(1)}, f32[1,32]{1,0:T(1,128)}, u32[]{:S(2)}) copy-start(f32[1,32]{1,0:T(1,128)} %weight_ref.1) | copy-start | bytes 388

commit v6 on v3

--- a/solution.py
+++ b/solution.py
@@ -11,14 +11,15 @@
 SIZES = (4, 2, 4, 4, 8)
 ROW, COL = ("z_hi", "core"), ("y", "x", "z_lo")
 VMEM = pl.BlockSpec(memory_space=pltpu.VMEM)
-T_STEP, S_STEP = 1024, 512
+SMEM = pl.BlockSpec(memory_space=pltpu.SMEM)
+S_STEP = 1024
 
 
-def kernel_call(body, outs, count, scratch=(), name=None, room=40):
+def kernel_call(body, outs, count, scratch=(), name=None, room=40, smem=0):
     return pl.pallas_call(
         body,
         out_shape=outs,
-        in_specs=[VMEM] * count,
+        in_specs=[SMEM] * smem + [VMEM] * (count - smem),
         out_specs=jax.tree.map(lambda _: VMEM, outs),
         scratch_shapes=list(scratch),
         name=name,
@@ -56,19 +57,35 @@
     probe_ref[...] = jnp.concatenate(columns, axis=0).astype(BF16)
 
 
-def image_kernel(strips_ref, unit_ref, probe_ref, out_ref, turned_ref):
-    turned_ref[...] = strips_ref[...].T
+def add_image(strips, unit_ref, probe_ref, half):
+    strip = strips[64 * half : 64 * half + 64, :]
+    total = jnp.zeros((16, 512), F32)
+    for number in range(2048 // S_STEP):
+        skus = slice(number * S_STEP, (number + 1) * S_STEP)
+        corr = jnp.dot(unit_ref[skus, :], strip, preferred_element_type=F32)
+        affinity = jnp.exp(corr).astype(BF16)
+        total = total + jnp.dot(probe_ref[:, skus], affinity, preferred_element_type=F32)
+    return total
+
+
+def own_kernel(strips_ref, unit_ref, probe_ref, out_ref):
+    turned = strips_ref[...].T
     for half in range(2):
-        for step in range(2048 // T_STEP):
-            strip = turned_ref[64 * half : 64 * half + 64, T_STEP * step : T_STEP * (step + 1)]
-            total = jnp.zeros((16, T_STEP), F32)
-            for number in range(2048 // S_STEP):
-                skus = slice(number * S_STEP, (number + 1) * S_STEP)
-                corr = jnp.dot(unit_ref[skus, :], strip, preferred_element_type=F32)
-                affinity = jnp.exp(corr).astype(BF16)
-                total = total + jnp.dot(probe_ref[:, skus], affinity, preferred_element_type=F32)
-            for k in range(T_STEP // 128):
-                out_ref[step * (T_STEP // 128) + k, 16 * half : 16 * half + 16, :] = total[:, 128 * k : 128 * (k + 1)]
+        total = add_image(turned, unit_ref, probe_ref, half)
+        for k in range(4):
+            out_ref[k, 16 * half : 16 * half + 16, :] = total[:, 128 * k : 128 * (k + 1)]
+
+
+def image_kernel(y_ref, strips_ref, unit_ref, probe_ref, own_ref, out_ref):
+    y = y_ref[0]
+    out_ref[pl.ds(4 * y, 4)] = own_ref[...]
+    for other in range(1, 4):
+        place = lax.rem(y + other, 4)
+        turned = strips_ref[pl.ds(pl.multiple_of(512 * place, 512), 512), :].T
+        for half in range(2):
+            total = add_image(turned, unit_ref, probe_ref, half)
+            for k in range(4):
+                out_ref[4 * place + k, 16 * half : 16 * half + 16, :] = total[:, 128 * k : 128 * (k + 1)]
 
 
 def turn_kernel(parts_ref, out_ref):
@@ -118,31 +135,43 @@
     out_ref[...] = left / jnp.sqrt(pivots)
 
 
+Z_LO_ORDER = [4, 0, 1, 2, 3, 5, 6, 7]
+X_Z_LO_ORDER = [8 * x + z for x in range(4) for z in Z_LO_ORDER]
+Z_ORDER = [16, 0] + [z for k in range(1, 16) for z in (32 - k, k)]
+
+
+def exchange(pieces, axes, order=None):
+    groups = None if order is None else [order]
+    return lax.all_to_all(pieces, axes, 0, 0, axis_index_groups=groups, tiled=True)
+
+
 def per_device(strip_factors, sku_factors, probe, demand_weight):
     strips, skus = kernel_call(
-        pack_kernel, (shape((8, 16, 128), BF16), shape((16, 1280), BF16)), 3, name="pack", room=63
+        pack_kernel, (shape((32, 16, 128), BF16), shape((16, 1280), BF16)), 3, name="pack", room=63
     )(strip_factors, sku_factors.T, probe.T)
     panel = lax.all_gather(skus, "z_hi", axis=0)
-    strips = lax.all_to_all(strips, "z_lo", 0, 0, tiled=True).reshape(128, 128)
+    strips = exchange(strips, ("x", "z_lo"), X_Z_LO_ORDER).reshape(512, 128)
     strips, panel = lax.optimization_barrier((strips, panel))
-    strips = jnp.broadcast_to(strips[None], (16, 128, 128))
-    strips = lax.all_to_all(strips, ("y", "x"), 0, 0, tiled=True).reshape(2048, 128)
+    own = strips
+    strips = exchange(jnp.broadcast_to(strips[None], (4, 512, 128)), "y").reshape(2048, 128)
     panel = lax.all_gather(panel, "core", axis=0)
     unit, columns = kernel_call(
         prepare_kernel, (shape((2048, 64), BF16), shape((16, 2048), BF16)), 1, name="prepare"
     )(panel)
-    total = kernel_call(
-        image_kernel, shape((16, 32, 128)), 3, name="image", scratch=[pltpu.VMEM((128, 2048), BF16)]
-    )(strips, unit, columns)
-    total = lax.all_to_all(total, ("y", "x"), 0, 0, tiled=True)
+    total = kernel_call(own_kernel, shape((4, 32, 128)), 3, name="own")(own, unit, columns)
+    place = jnp.full((1,), lax.axis_index("y"), jnp.int32)
+    total = kernel_call(image_kernel, shape((16, 32, 128)), 5, smem=1, name="image")(
+        place, strips, unit, columns, total
+    )
+    total = exchange(total, ("y", "x"))
     total = kernel_call(turn_kernel, shape((8, 4, 128)), 1, name="turn")(total)
-    total = lax.all_to_all(total, "z_lo", 0, 0, tiled=True)
+    total = exchange(total, "z_lo", Z_LO_ORDER)
     image, gram = kernel_call(
         gram_kernel, (shape((16, 32)), shape((32, 2, 128))), 2, name="gram"
     )(total, demand_weight)
-    gram = lax.all_to_all(gram, ("core", "y", "x"), 0, 0, tiled=True)
+    gram = exchange(gram, ("core", "y", "x"))
     gram = kernel_call(sum_kernel, shape((32, 2, 128)), 1, name="sum")(gram)
-    gram = lax.all_to_all(gram, ("z_hi", "z_lo"), 0, 0, tiled=True)
+    gram = exchange(gram, ("z_hi", "z_lo"), Z_ORDER)
     return kernel_call(basis_kernel, shape((16, 32)), 2, name="basis")(gram, image)
 
 

time: 158 us -> 140 us (0.89)
  blocking collectives: 122 us -> 107 us
  waiting for transfers between devices: 3.08 us -> 0.01 us
    all_to_all x4, blocking collectives: 81.9 us -> 64.3 us  [exchange(): lax.all_to_all(pieces, axes, 0, 0, axis_index_groups=groups, tiled=True)]
    all_to_all x2, waiting for transfers between devices: 3.08 us -> 0.01 us  [exchange(): lax.all_to_all(pieces, axes, 0, 0, axis_index_groups=groups, tiled=True)]
    all_gather x1, blocking collectives: 34.5 us -> 36.6 us  [per_device(): panel = lax.all_gather(skus, 'z_hi', axis=0)]
    pallas_call x2 -> x3, Pallas kernels: 8.28 us -> 8.49 us  [the longest x1 5.09 us: per_device(): kernel_call(image_kernel, shape((16, 32, 128)), 5, smem=1, name='image')]
  transfers between devices with their start and end apart: 2 -> 2, of which waited for: 1 -> 0; matrix products, arithmetic and copies ran while one was open for 0% -> 0% of each run, Pallas kernels for 0% -> 1%
where the time goes in v6:
time: 140 us
  blocking collectives  107 us (76%)
  starting transfers between devices  20.3 us (14%)
  Pallas kernels  11.4 us (8%)
    all_to_all x4, blocking collectives, exchange(): lax.all_to_all(pieces, axes, 0, 0, axis_index_groups=groups, tiled=True)  64.3 us
    all_gather x1, blocking collectives, per_device(): panel = lax.all_gather(skus, 'z_hi', axis=0)  36.6 us
    all_to_all x2, starting transfers between devices, exchange(): lax.all_to_all(pieces, axes, 0, 0, axis_index_groups=groups, tiled=True)  20.3 us
    all_gather x1, blocking collectives, per_device(): panel = lax.all_gather(panel, 'core', axis=0)  6.42 us
    pallas_call x1, Pallas kernels, per_device(): kernel_call(image_kernel, shape((16, 32, 128)), 5, smem=1, name='image')  5.09 us
  transfers between devices with their start and end apart: 2, of which 0 were waited for; matrix products, arithmetic and copies ran while one was open for 0% of the time, Pallas kernels for 1%

profile of v6, /device:TPU:1, one launch (start us, length us, event | category | flops | bytes accessed | tf_op | source)
XLA Modules:
  0.0 139.9 jit_solution(6075897655023027681)
XLA Ops:
  0.0 1.6 %pack.1 = (bf16[32,16,128]{2,1,0:T(8,128)(2,1)}, bf16[16,1280]{1,0:T(8,128)(2,1)}) custom-call(bf16[32,64]{1,0:T(8,128)(2,1)} %strip_ref.1, bf16[8,2048]{1,0:T(8,128)(2,1)} %bitcast.12, bf16[2,2048]{1,0:T(2,128)(2,1)} %bitcast.13), custom_call_target="tpu_custom_call" | custom-call | tf_op jit(solution)/shard_map/pack/pallas_call | solution.py:149
  1.6 0.0 copy-start.1
  1.6 16.1 %all-to-all-start = ((bf16[32,16,128]{2,1,0:T(8,128)(2,1)}), bf16[32,16,128]{2,1,0:T(8,128)(2,1)S(1)}, u32[]{:S(2)}, u32[]{:S(2)}) async-start(bf16[32,16,128]{2,1,0:T(8,128)(2,1)} %get-tuple-element.13), calls=%async_computation | async-start | bytes 262144 | tf_op jit(solution)/shard_map/all_to_all | solution.py:145
  17.7 0.0 copy-done.1
  17.7 36.6 %all-gather = bf16[64,1280]{1,0:T(8,128)(2,1)S(1)} all-gather(bf16[16,1280]{1,0:T(8,128)(2,1)S(1)} %copy-done.1), channel_id=2, replica_groups=mesh['z_hi'=4,'core'=2,'y'=4,'x'=4,'z_lo'=8] {'z_hi'}, dimensions={0}, use_global_device_ids=true | all-gather | bytes 204800 | tf_op jit(solution)/shard_map/all_gather | solution.py:152
  54.3 0.0 all-to-all-done
  54.3 0.9 broadcast_in_dim.10
  55.2 4.2 %all-to-all-start.1 = ((bf16[4,512,128]{2,1,0:T(8,128)(2,1)}), bf16[4,512,128]{2,1,0:T(8,128)(2,1)S(1)}, u32[]{:S(2)}, u32[]{:S(2)}) async-start(bf16[4,512,128]{2,1,0:T(8,128)(2,1)} %broadcast_in_dim.10), calls=%async_computation.1 | async-start | bytes 1048576 | tf_op jit(solution)/shard_map/all_to_all | solution.py:145
  59.4 6.4 %all-gather.1 = bf16[8,16,1280]{2,1,0:T(8,128)(2,1)S(1)} all-gather(bf16[4,16,1280]{2,1,0:T(8,128)(2,1)S(1)} %bitcast.11), channel_id=3, replica_groups=mesh['z_hi'=4,'core'=2,'y'=4,'x'=4,'z_lo'=8] {'core'}, dimensions={0}, use_global_device_ids=true | all-gather | bytes 491520 | tf_op jit(solution)/shard_map/all_gather | solution.py:157
  65.8 0.2 prepare.1
  66.0 1.8 %own.1.own_ref = f32[4,32,128]{2,1,0:T(8,128)S(1)} custom-call(bf16[512,128]{1,0:T(8,128)(2,1)S(1)} %bitcast.10, bf16[2048,64]{1,0:T(8,128)(2,1)S(1)} %get-tuple-element.17.unit_ref, bf16[16,2048]{1,0:T(8,128)(2,1)S(1)} %get-tuple-element.18.probe_ref), custom_call_target="tpu_custom_call" | custom-call | tf_op jit(solution)/shard_map/own/pallas_call | solution.py:161
  67.8 0.0 all-to-all-done.1
  67.8 5.1 %image.1 = f32[16,32,128]{2,1,0:T(8,128)S(1)} custom-call(s32[1]{0:T(128)} %bitcast.y_ref, bf16[2048,128]{1,0:T(8,128)(2,1)S(1)} %bitcast.7, bf16[2048,64]{1,0:T(8,128)(2,1)S(1)} %get-tuple-element.17.unit_ref, bf16[16,2048]{1,0:T(8,128)(2,1)S(1)} %get-tuple-element.18.probe_ref, f32[4,32,128]{2,1,0:T(8,128)S(1)} %own.1.own_ref), custom_call_target="tpu_custom_call" | custom-call | tf_op jit(solution)/shard_map/image/pallas_call | solution.py:163
  72.9 14.6 %all_to_all.30.parts_ref = f32[16,32,128]{2,1,0:T(8,128)S(1)} all-to-all(f32[16,32,128]{2,1,0:T(8,128)S(1)} %image.1), channel_id=1, replica_groups=mesh['z_hi'=4,'core'=2,'y'=4,'x'=4,'z_lo'=8] {'y','x'}, dimensions={0} | all-to-all | bytes 524288 | tf_op jit(solution)/shard_map/all_to_all | solution.py:145
  87.6 0.2 turn.1
  87.8 0.0 copy-start
  87.8 10.7 %all_to_all.31.parts_ref = f32[8,4,128]{2,1,0:T(4,128)S(1)} all-to-all(f32[8,4,128]{2,1,0:T(4,128)S(1)} %turn.1), channel_id=1, replica_groups={{4,0,1,2,3,5,6,7},{12,8,9,10,11,13,14,15},{20,16,17,18,19,21,22,23},{28..., dimensions={0} | all-to-all | bytes 32768 | tf_op jit(solution)/shard_map/all_to_all | solution.py:145
  98.5 0.0 copy-done
  98.5 0.4 gram.1
  98.9 14.8 %all_to_all.32.parts_ref = f32[32,2,128]{2,1,0:T(2,128)S(1)} all-to-all(f32[32,2,128]{2,1,0:T(2,128)S(1)} %get-tuple-element.19), channel_id=1, replica_groups=mesh['z_hi'=4,'core'=2,'y'=4,'x'=4,'z_lo'=8] {'core','y','x'}, dimensions={0} | all-to-all | bytes 65536 | tf_op jit(solution)/shard_map/all_to_all | solution.py:145
  113.7 24.2 %all_to_all.33.parts_ref = f32[32,2,128]{2,1,0:T(2,128)S(1)} all-to-all(f32[32,2,128]{2,1,0:T(2,128)S(1)} %sum.1), channel_id=1, replica_groups={{512,0,775,1,774,2,773,3,772,4,771,5,770,6,769,7,768,256,519,257,518,25..., dimensions={0} | all-to-all | bytes 65536 | tf_op jit(solution)/shard_map/all_to_all | solution.py:145
  137.9 2.0 %basis.1 = f32[16,32]{1,0:T(8,128)} custom-call(f32[32,2,128]{2,1,0:T(2,128)S(1)} %all_to_all.33.parts_ref, f32[16,32]{1,0:T(8,128)S(1)} %get-tuple-element.20.image_ref), custom_call_target="tpu_custom_call" | custom-call | tf_op jit(solution)/shard_map/basis/pallas_call | solution.py:175
  (1 shorter events, 0.0 us)
Async XLA Ops:
  1.6 16.1 %copy-start.1 = (bf16[16,1280]{1,0:T(8,128)(2,1)S(1)}, bf16[16,1280]{1,0:T(8,128)(2,1)}, u32[]{:S(2)}) copy-start(bf16[16,1280]{1,0:T(8,128)(2,1)} %get-tuple-element.14) | copy-start | bytes 122884
  1.6 52.7 %all-to-all-start = ((bf16[32,16,128]{2,1,0:T(8,128)(2,1)}), bf16[32,16,128]{2,1,0:T(8,128)(2,1)S(1)}, u32[]{:S(2)}, u32[]{:S(2)}) async-start(bf16[32,16,128]{2,1,0:T(8,128)(2,1)} %get-tuple-element.13), calls=%async_computation | async-start | bytes 262144 | tf_op jit(solution)/shard_map/all_to_all | solution.py:145
  55.2 12.7 %all-to-all-start.1 = ((bf16[4,512,128]{2,1,0:T(8,128)(2,1)}), bf16[4,512,128]{2,1,0:T(8,128)(2,1)S(1)}, u32[]{:S(2)}, u32[]{:S(2)}) async-start(bf16[4,512,128]{2,1,0:T(8,128)(2,1)} %broadcast_in_dim.10), calls=%async_computation.1 | async-start | bytes 1048576 | tf_op jit(solution)/shard_map/all_to_all | solution.py:145
  87.8 10.7 %copy-start = (f32[1,32]{1,0:T(1,128)S(1)}, f32[1,32]{1,0:T(1,128)}, u32[]{:S(2)}) copy-start(f32[1,32]{1,0:T(1,128)} %weight_ref.1) | copy-start | bytes 388

commit v7 on v6

--- a/solution.py
+++ b/solution.py
@@ -135,7 +135,7 @@
     out_ref[...] = left / jnp.sqrt(pivots)
 
 
-Z_LO_ORDER = [4, 0, 1, 2, 3, 5, 6, 7]
+Z_LO_ORDER = [3, 0, 1, 2, 4, 5, 6, 7]
 X_Z_LO_ORDER = [8 * x + z for x in range(4) for z in Z_LO_ORDER]
 Z_ORDER = [16, 0] + [z for k in range(1, 16) for z in (32 - k, k)]
 

time: 140 us -> 141 us (level)
    all_gather x1, blocking collectives: 36.6 us -> 34.6 us  [per_device(): panel = lax.all_gather(skus, 'z_hi', axis=0)]
    all_to_all x4, blocking collectives: 64.3 us -> 66 us  [exchange(): lax.all_to_all(pieces, axes, 0, 0, axis_index_groups=groups, tiled=True)]
where the time goes in v7:
time: 141 us; the launch traced here: 140 us
  blocking collectives  108 us (77%)
  starting transfers between devices  20.3 us (14%)
  Pallas kernels  11.4 us (8%)
    all_to_all x4, blocking collectives, exchange(): lax.all_to_all(pieces, axes, 0, 0, axis_index_groups=groups, tiled=True)  66 us
    all_gather x1, blocking collectives, per_device(): panel = lax.all_gather(skus, 'z_hi', axis=0)  34.6 us
    all_to_all x2, starting transfers between devices, exchange(): lax.all_to_all(pieces, axes, 0, 0, axis_index_groups=groups, tiled=True)  20.3 us
    all_gather x1, blocking collectives, per_device(): panel = lax.all_gather(panel, 'core', axis=0)  7.15 us
    pallas_call x1, Pallas kernels, per_device(): kernel_call(image_kernel, shape((16, 32, 128)), 5, smem=1, name='image')  5.1 us
  transfers between devices with their start and end apart: 2, of which 0 were waited for; matrix products, arithmetic and copies ran while one was open for 0% of the time, Pallas kernels for 1%

profile of v7, /device:TPU:1, one launch (start us, length us, event | category | flops | bytes accessed | tf_op | source)
XLA Modules:
  0.0 140.3 jit_solution(15431782656521234447)
XLA Ops:
  0.0 1.6 %pack.1 = (bf16[32,16,128]{2,1,0:T(8,128)(2,1)}, bf16[16,1280]{1,0:T(8,128)(2,1)}) custom-call(bf16[32,64]{1,0:T(8,128)(2,1)} %strip_ref.1, bf16[8,2048]{1,0:T(8,128)(2,1)} %bitcast.12, bf16[2,2048]{1,0:T(2,128)(2,1)} %bitcast.13), custom_call_target="tpu_custom_call" | custom-call | tf_op jit(solution)/shard_map/pack/pallas_call | solution.py:149
  1.6 0.0 copy-start.1
  1.6 16.1 %all-to-all-start = ((bf16[32,16,128]{2,1,0:T(8,128)(2,1)}), bf16[32,16,128]{2,1,0:T(8,128)(2,1)S(1)}, u32[]{:S(2)}, u32[]{:S(2)}) async-start(bf16[32,16,128]{2,1,0:T(8,128)(2,1)} %get-tuple-element.13), calls=%async_computation | async-start | bytes 262144 | tf_op jit(solution)/shard_map/all_to_all | solution.py:145
  17.7 0.0 copy-done.1
  17.7 34.6 %all-gather = bf16[64,1280]{1,0:T(8,128)(2,1)S(1)} all-gather(bf16[16,1280]{1,0:T(8,128)(2,1)S(1)} %copy-done.1), channel_id=2, replica_groups=mesh['z_hi'=4,'core'=2,'y'=4,'x'=4,'z_lo'=8] {'z_hi'}, dimensions={0}, use_global_device_ids=true | all-gather | bytes 204800 | tf_op jit(solution)/shard_map/all_gather | solution.py:152
  52.3 0.0 all-to-all-done
  52.3 0.9 broadcast_in_dim.10
  53.2 4.2 %all-to-all-start.1 = ((bf16[4,512,128]{2,1,0:T(8,128)(2,1)}), bf16[4,512,128]{2,1,0:T(8,128)(2,1)S(1)}, u32[]{:S(2)}, u32[]{:S(2)}) async-start(bf16[4,512,128]{2,1,0:T(8,128)(2,1)} %broadcast_in_dim.10), calls=%async_computation.1 | async-start | bytes 1048576 | tf_op jit(solution)/shard_map/all_to_all | solution.py:145
  57.4 7.1 %all-gather.1 = bf16[8,16,1280]{2,1,0:T(8,128)(2,1)S(1)} all-gather(bf16[4,16,1280]{2,1,0:T(8,128)(2,1)S(1)} %bitcast.11), channel_id=3, replica_groups=mesh['z_hi'=4,'core'=2,'y'=4,'x'=4,'z_lo'=8] {'core'}, dimensions={0}, use_global_device_ids=true | all-gather | bytes 491520 | tf_op jit(solution)/shard_map/all_gather | solution.py:157
  64.5 0.2 prepare.1
  64.7 1.8 %own.1.own_ref = f32[4,32,128]{2,1,0:T(8,128)S(1)} custom-call(bf16[512,128]{1,0:T(8,128)(2,1)S(1)} %bitcast.10, bf16[2048,64]{1,0:T(8,128)(2,1)S(1)} %get-tuple-element.17.unit_ref, bf16[16,2048]{1,0:T(8,128)(2,1)S(1)} %get-tuple-element.18.probe_ref), custom_call_target="tpu_custom_call" | custom-call | tf_op jit(solution)/shard_map/own/pallas_call | solution.py:161
  66.6 0.0 all-to-all-done.1
  66.6 5.1 %image.1 = f32[16,32,128]{2,1,0:T(8,128)S(1)} custom-call(s32[1]{0:T(128)} %bitcast.y_ref, bf16[2048,128]{1,0:T(8,128)(2,1)S(1)} %bitcast.7, bf16[2048,64]{1,0:T(8,128)(2,1)S(1)} %get-tuple-element.17.unit_ref, bf16[16,2048]{1,0:T(8,128)(2,1)S(1)} %get-tuple-element.18.probe_ref, f32[4,32,128]{2,1,0:T(8,128)S(1)} %own.1.own_ref), custom_call_target="tpu_custom_call" | custom-call | tf_op jit(solution)/shard_map/image/pallas_call | solution.py:163
  71.7 13.5 %all_to_all.30.parts_ref = f32[16,32,128]{2,1,0:T(8,128)S(1)} all-to-all(f32[16,32,128]{2,1,0:T(8,128)S(1)} %image.1), channel_id=1, replica_groups=mesh['z_hi'=4,'core'=2,'y'=4,'x'=4,'z_lo'=8] {'y','x'}, dimensions={0} | all-to-all | bytes 524288 | tf_op jit(solution)/shard_map/all_to_all | solution.py:145
  85.1 0.2 turn.1
  85.3 0.0 copy-start
  85.4 13.5 %all_to_all.31.parts_ref = f32[8,4,128]{2,1,0:T(4,128)S(1)} all-to-all(f32[8,4,128]{2,1,0:T(4,128)S(1)} %turn.1), channel_id=1, replica_groups={{3,0,1,2,4,5,6,7},{11,8,9,10,12,13,14,15},{19,16,17,18,20,21,22,23},{27..., dimensions={0} | all-to-all | bytes 32768 | tf_op jit(solution)/shard_map/all_to_all | solution.py:145
  98.9 0.0 copy-done
  98.9 0.4 gram.1
  99.3 14.8 %all_to_all.32.parts_ref = f32[32,2,128]{2,1,0:T(2,128)S(1)} all-to-all(f32[32,2,128]{2,1,0:T(2,128)S(1)} %get-tuple-element.19), channel_id=1, replica_groups=mesh['z_hi'=4,'core'=2,'y'=4,'x'=4,'z_lo'=8] {'core','y','x'}, dimensions={0} | all-to-all | bytes 65536 | tf_op jit(solution)/shard_map/all_to_all | solution.py:145
  114.1 24.2 %all_to_all.33.parts_ref = f32[32,2,128]{2,1,0:T(2,128)S(1)} all-to-all(f32[32,2,128]{2,1,0:T(2,128)S(1)} %sum.1), channel_id=1, replica_groups={{512,0,775,1,774,2,773,3,772,4,771,5,770,6,769,7,768,256,519,257,518,25..., dimensions={0} | all-to-all | bytes 65536 | tf_op jit(solution)/shard_map/all_to_all | solution.py:145
  138.4 2.0 %basis.1 = f32[16,32]{1,0:T(8,128)} custom-call(f32[32,2,128]{2,1,0:T(2,128)S(1)} %all_to_all.33.parts_ref, f32[16,32]{1,0:T(8,128)S(1)} %get-tuple-element.20.image_ref), custom_call_target="tpu_custom_call" | custom-call | tf_op jit(solution)/shard_map/basis/pallas_call | solution.py:175
  (1 shorter events, 0.0 us)
Async XLA Ops:
  1.6 16.1 %copy-start.1 = (bf16[16,1280]{1,0:T(8,128)(2,1)S(1)}, bf16[16,1280]{1,0:T(8,128)(2,1)}, u32[]{:S(2)}) copy-start(bf16[16,1280]{1,0:T(8,128)(2,1)} %get-tuple-element.14) | copy-start | bytes 122884
  1.6 50.7 %all-to-all-start = ((bf16[32,16,128]{2,1,0:T(8,128)(2,1)}), bf16[32,16,128]{2,1,0:T(8,128)(2,1)S(1)}, u32[]{:S(2)}, u32[]{:S(2)}) async-start(bf16[32,16,128]{2,1,0:T(8,128)(2,1)} %get-tuple-element.13), calls=%async_computation | async-start | bytes 262144 | tf_op jit(solution)/shard_map/all_to_all | solution.py:145
  53.2 13.4 %all-to-all-start.1 = ((bf16[4,512,128]{2,1,0:T(8,128)(2,1)}), bf16[4,512,128]{2,1,0:T(8,128)(2,1)S(1)}, u32[]{:S(2)}, u32[]{:S(2)}) async-start(bf16[4,512,128]{2,1,0:T(8,128)(2,1)} %broadcast_in_dim.10), calls=%async_computation.1 | async-start | bytes 1048576 | tf_op jit(solution)/shard_map/all_to_all | solution.py:145
  85.3 13.5 %copy-start = (f32[1,32]{1,0:T(1,128)S(1)}, f32[1,32]{1,0:T(1,128)}, u32[]{:S(2)}) copy-start(f32[1,32]{1,0:T(1,128)} %weight_ref.1) | copy-start | bytes 388
